TPU v7x, 256 devices: a whole 4x4x8 slice. The times are simulated.
256 devices in a mesh: dp: 64 (over x, y_hi, z), mp: 4 (over y_lo, core).
Axes of the slice: x: 4, y: 4 (y_hi: 2, y_lo: 2; y = y_hi * 2 + y_lo), z: 8, core: 2. Of those that a mesh axis runs over, the one named last changes fastest.
Arguments:
- images: bfloat16 [128, 729, 1152], P('dp', None, 'mp'), may hold values from -8 to 8
- ln_gain: float32 [1152], replicated, may hold values from 0.1 to 1.9
- w_in: bfloat16 [1152, 4304], P(None, 'mp'), may hold values from -0.1875 to 0.1875
- b_in: float32 [4304], P('mp'), may hold values from -3 to 3
- w_out: bfloat16 [4304, 1152], P('mp'), may hold values from -0.09375 to 0.09375
- texts: bfloat16 [128, 1152], P('dp'), may hold values from -6 to 6
- w_text: bfloat16 [1152, 1152], replicated, may hold values from -0.1875 to 0.1875
- b_text: float32 [1152], replicated, may hold values from -3 to 3
- logit_scale: float32 [1], replicated, may hold values from 8 to 32
- logit_bias: float32 [1], replicated, may hold values from -4 to 0
Outputs:
- grad_w_in: float32 [1152, 4304], P('dp', 'mp')
- grad_w_out: float32 [4304, 1152], P('mp', 'dp')
- grad_w_text: float32 [1152, 1152], P('dp')
- grad_texts: bfloat16 [128, 1152], P('dp')
All inputs are finite; a program needn't handle non-finite values.
Results may differ from a plain program's by a relative error of at most 0.011.
Values may be sent and summed in bfloat16 or wider, within the bound.
A program may use at most 128 MiB of HBM per device.

v0:
```python
import jax
import jax.numpy as jnp
from jax import lax
from jax.sharding import PartitionSpec as P

sqrt_two_pi = 0.7978845608028654
cubic_term = 0.044715
epsilon = 1e-06


def gelu_tanh(values):
    return (
        0.5
        * values
        * (1.0 + jnp.tanh(sqrt_two_pi * (values + cubic_term * values * values * values)))
    )


def gelu_slope(values):
    tanh_part = jnp.tanh(sqrt_two_pi * (values + cubic_term * values * values * values))
    return 0.5 * (1.0 + tanh_part) + 0.5 * values * (1.0 - tanh_part * tanh_part) * sqrt_two_pi * (
        1.0 + 3.0 * cubic_term * values * values
    )


def layer_norm(image_rows, ln_gain):
    values = image_rows.astype(jnp.float32)
    centered = values - jnp.mean(values, axis=-1, keepdims=True)
    spread = jnp.mean(centered * centered, axis=-1, keepdims=True)
    return (centered * lax.rsqrt(spread + epsilon) * ln_gain).astype(jnp.bfloat16)


def contract_rows(left_side, right_side, precision=None):
    return lax.dot_general(
        left_side,
        right_side,
        (((0,), (0,)), ((), ())),
        preferred_element_type=jnp.float32,
        precision=precision,
    )


def pair_weights(logits, matches, logit_scale):
    pair_signs = jnp.where(matches, 1.0, -1.0)
    pair_coef = -pair_signs * jax.nn.sigmoid(-pair_signs * logits)
    return (logit_scale[0] * pair_coef).astype(jnp.bfloat16)


def shards(images, ln_gain, w_in, b_in, w_out, texts, w_text, b_text, logit_scale, logit_bias):
    image_count, patch_count, shard_width = images.shape
    full_images = lax.all_gather(images, "mp", axis=2, tiled=True)
    model_width = full_images.shape[2]
    hidden_part = w_in.shape[1]
    row_total = image_count * patch_count
    normed = layer_norm(full_images.reshape(row_total, model_width), ln_gain)
    before = jnp.dot(normed, w_in, preferred_element_type=jnp.float32) + b_in
    activated = gelu_tanh(before).astype(jnp.bfloat16)
    partial_out = jnp.dot(activated, w_out, preferred_element_type=jnp.float32).reshape(
        image_count, patch_count, model_width
    )
    summed = lax.psum_scatter(
        partial_out.astype(jnp.bfloat16), "mp", scatter_dimension=2, tiled=True
    ).astype(jnp.float32)
    local_pooled = jnp.mean(images.astype(jnp.float32) + summed, axis=1)
    pooled = lax.all_gather(local_pooled, "mp", axis=1, tiled=True)
    act_sum = jnp.sum(
        activated.reshape(image_count, patch_count, hidden_part), axis=1, dtype=jnp.float32
    )
    image_norm = jnp.sqrt(jnp.sum(pooled * pooled, axis=1, keepdims=True) + epsilon)
    image_unit = pooled / image_norm
    image_emb = image_unit.astype(jnp.bfloat16)
    text_proj = jnp.dot(texts, w_text, preferred_element_type=jnp.float32) + b_text
    text_norm = jnp.sqrt(jnp.sum(text_proj * text_proj, axis=1, keepdims=True) + epsilon)
    text_unit = text_proj / text_norm
    text_emb = text_unit.astype(jnp.bfloat16)
    all_text = lax.all_gather(text_emb, "dp", axis=0, tiled=True)
    batch_total = all_text.shape[0]
    first_image = lax.axis_index("dp") * image_count
    own_index = first_image + jnp.arange(image_count, dtype=jnp.int32)
    logits = (
        logit_scale[0] * jnp.dot(image_emb, all_text.T, preferred_element_type=jnp.float32)
        + logit_bias[0]
    )
    matches = own_index[:, None] == jnp.arange(batch_total, dtype=jnp.int32)[None, :]
    scaled = pair_weights(logits, matches, logit_scale)
    grad_image_emb = jnp.dot(scaled, all_text, preferred_element_type=jnp.float32)
    columns = scaled
    grad_text_emb = lax.psum_scatter(
        contract_rows(columns, image_emb), "dp", scatter_dimension=0, tiled=True
    )
    grad_pooled = (
        grad_image_emb - image_unit * jnp.sum(image_unit * grad_image_emb, axis=1, keepdims=True)
    ) / image_norm
    grad_block = (grad_pooled / patch_count).astype(jnp.bfloat16)
    grad_act = lax.dot_general(
        grad_block, w_out, (((1,), (1,)), ((), ())), preferred_element_type=jnp.float32
    )
    gelu_grad = gelu_slope(before).reshape(image_count, patch_count, hidden_part)
    grad_pre = (
        (grad_act[:, None, :] * gelu_grad).astype(jnp.bfloat16).reshape(row_total, hidden_part)
    )
    grad_text_proj = (
        (grad_text_emb - text_unit * jnp.sum(text_unit * grad_text_emb, axis=1, keepdims=True))
        / text_norm
    ).astype(jnp.bfloat16)
    grad_texts = lax.dot_general(
        grad_text_proj, w_text, (((1,), (1,)), ((), ())), preferred_element_type=jnp.float32
    ).astype(jnp.bfloat16)
    columns = normed
    first_part = contract_rows(columns, grad_pre)
    block_cols = grad_block.astype(jnp.float32)
    block_part = contract_rows(block_cols, act_sum, lax.Precision.HIGHEST)
    text_part = contract_rows(texts, grad_text_proj)
    summed_grads = lax.psum_scatter(
        jnp.concatenate([first_part, block_part, text_part], axis=1),
        "dp",
        scatter_dimension=0,
        tiled=True,
    )
    grad_w_in = summed_grads[:, :hidden_part]
    grad_w_out = summed_grads[:, hidden_part : 2 * hidden_part].T
    grad_w_text = summed_grads[:, 2 * hidden_part :]
    return (grad_w_in, grad_w_out, grad_w_text, grad_texts)


def solution(mesh):
    placed = (
        P("dp", None, "mp"),
        P(),
        P(None, "mp"),
        P("mp"),
        P("mp", None),
        P("dp", None),
        P(),
        P(),
        P(),
        P(),
    )
    return jax.shard_map(
        shards,
        mesh=mesh,
        in_specs=placed,
        out_specs=(P("dp", "mp"), P("mp", "dp"), P("dp", None), P("dp", None)),
        check_vma=False,
    )
```

profile of v0, /device:TPU:8, one launch (start us, length us, event | category | flops | bytes accessed | tf_op | source)
XLA Modules:
  0.0 1808.4 jit_solution(6270998722018543832)
XLA Ops:
  8.0 46.7 %all-gather.4.cloned.1.call-done = bf16[2,729,1152]{1,2,0:T(8,128)(2,1)} async-done(((bf16[2,729,288]{1,2,0:T(8,128)(2,1)}), bf16[2,729,1152]{1,2,0:T(8,128)(2,1)}) %all-gather.4.cloned.1.call-update) | async-done | bytes 3359248 | tf_op jit(solution)/shard_map/all_gather | solution.py:51
  54.7 6.0 copy.42
  60.7 6.4 reshape.73
  67.1 2.6 convert_reduce_fusion
  69.8 3.0 multiply_reduce_fusion
  72.9 11.1 fusion.33
  84.0 2.8 copy-done.18
  86.8 7.0 convolution_convert_fusion
  93.8 4.4 convert_element_type.64
  98.2 10.6 copy.43
  109.5 184.3 %all-gather.1 = bf16[64,2,1152]{2,1,0:T(2,128)(2,1)S(1)} all-gather(bf16[1,2,1152]{2,1,0:T(2,128)(2,1)S(1)} %get-tuple-element.24), channel_id=1, replica_groups=mesh['dp'=64,'mp'=4] {'dp'}, dimensions={0}, use_global_device_ids=true | all-gather | bytes 299520 | tf_op jit(solution)/shard_map/all_gather | solution.py:76
  299.1 10.0 reshape.74
  309.1 19.0 %reduce_sum.78 = f32[2,1076]{0,1:T(8,128)} reduce(f32[2,729,1076]{1,0,2:T(2,128)} %reshape.74, f32[]{:T(128)} %constant.13.clone.1), dimensions={1}, to_apply=%region_7.8 | reduce | flops 1566656 | bytes 6283844 | tf_op jit(solution)/shard_map/reduce_sum | solution.py:66
  328.1 1.8 constant_dynamic-slice_fusion.1
  330.4 5.2 all-gather
  335.8 1.2 fusion.17
  337.0 1.3 fusion.18
  338.3 1.2 fusion.22
  339.4 2.6 fusion.30
  342.1 5.0 mul.147
  347.1 9.7 mul.148
  357.1 16.7 fusion.7
  373.8 4.7 fusion.29
  378.5 616.0 %all-reduce.9.cloned.1.call-done = f32[128,1152]{1,0:T(8,128)} async-done(((f32[128,1152]{1,0:T(8,128)}), f32[128,1152]{1,0:T(8,128)}) %all-reduce.9.cloned.1.call-update) | async-done | bytes 589840
  994.5 0.9 multiply_reduce_fusion.2
  995.4 4.0 convolution_bitcast_fusion
  999.4 38.9 %concatenate.3 = f32[1152,3304]{0,1:T(8,128)} concatenate(f32[1152,1076]{0,1:T(8,128)} %fusion.7, f32[1152,1076]{0,1:T(8,128)} %fusion.29, f32[1152,1152]{0,1:T(8,128)} %convolution_bitcast_fusion), dimensions={1} | concatenate | bytes 30449664 | tf_op jit(solution)/shard_map/concatenate | solution.py:115
  1039.0 2.2 convolution_convert_fusion.1
  1041.2 752.8 %all-reduce.11.cloned.1.call-done = f32[1152,3304]{0,1:T(8,128)} async-done(((f32[1152,3304]{0,1:T(8,128)}), f32[1152,3304]{0,1:T(8,128)}) %all-reduce.11.cloned.1.call-update) | async-done | bytes 15224848
  1794.0 2.7 dynamic-slice_bitcast_fusion
  1796.7 1.9 copy.49
  1799.5 1.5 dynamic-slice.8
  (67 shorter events, 7.1 us)
Async XLA Ops:
  7.2 101.7 %copy-start = (bf16[1152,1152]{1,0:T(8,128)(2,1)S(1)}, bf16[1152,1152]{1,0:T(8,128)(2,1)}, u32[]{:S(2)}) copy-start(bf16[1152,1152]{1,0:T(8,128)(2,1)} %param.16) | copy-start | bytes 7962628
  7.2 47.5 %all-gather.4.cloned.1.call-start = ((), (), s32[]{:S(2)}) async-start(), calls=%async_computation | async-start | bytes 4423680 | tf_op jit(solution)/shard_map/all_gather | solution.py:51
  7.9 320.1 %all-reduce.7.cloned.1.call-start = ((), (), s32[]{:S(2)}) async-start(), calls=%async_computation.1 | async-start | bytes 7077888
  67.1 5.8 copy-start.13
  67.1 5.8 copy-start.14
  69.8 14.2 copy-start.6
  72.9 11.1 copy-start.8
  72.9 13.9 copy-start.12
  84.0 2.8 copy-start.18
  98.2 10.7 copy-start.3
  98.2 10.7 copy-start.5
  98.2 197.8 %copy-start.17 = (u32[256]{0:T(256)S(1)}, u32[256]{0:T(256)}, u32[]{:S(2)}) copy-start(u32[256]{0:T(256)} %constant.40) | copy-start | bytes 3076
  98.2 198.4 %copy-start.16 = (u32[256]{0:T(256)S(1)}, u32[256]{0:T(256)}, u32[]{:S(2)}) copy-start(u32[256]{0:T(256)} %constant.44) | copy-start | bytes 3076
  108.8 885.7 %all-reduce.9.cloned.1.call-start = ((), (), s32[]{:S(2)}) async-start(), calls=%async_computation.2 | async-start | bytes 1179648
  109.5 189.6 %copy-start.10 = (f32[2]{0:T(128)}, f32[2]{0:T(128)S(1)}, u32[]{:S(2)}) copy-start(f32[2]{0:T(128)S(1)} %add_sqrt_fusion) | copy-start | bytes 28
  309.1 20.8 %copy-start.1 = (bf16[2,729,288]{1,2,0:T(8,128)(2,1)S(1)}, bf16[2,729,288]{1,2,0:T(8,128)(2,1)}, u32[]{:S(2)}) copy-start(bf16[2,729,288]{1,2,0:T(8,128)(2,1)} %param.10) | copy-start | bytes 2519428
  347.1 10.0 copy-start.7
  347.1 10.0 copy-start.9
  347.1 10.0 copy-start.15
  356.7 17.0 copy-start.2
  356.8 1437.3 %all-reduce.11.cloned.1.call-start = ((), (), s32[]{:S(2)}) async-start(), calls=%async_computation.3 | async-start | bytes 30449664
  373.8 621.6 %copy-start.4 = (bf16[2,1152]{1,0:T(2,128)(2,1)S(1)}, bf16[2,1152]{1,0:T(2,128)(2,1)}, u32[]{:S(2)}) copy-start(bf16[2,1152]{1,0:T(2,128)(2,1)} %param.15) | copy-start | bytes 13828
  373.8 621.6 %copy-start.11 = (f32[2]{0:T(128)S(1)}, f32[2]{0:T(128)}, u32[]{:S(2)}) copy-start(f32[2]{0:T(128)} %copy-done.10) | copy-start | bytes 28
Sparse Core Ops, SparseCore 0:
  9.8 44.7 all-gather.3
  108.9 87.5 all-reduce.6
  356.9 637.5 all-reduce.8
  1038.4 755.5 all-reduce.10
where the time goes:
time: 1810 us
  waiting for transfers between devices  1420 us (78%)
  blocking collectives  189 us (10%)
  local copies, waits for them, and re-layouts  106 us (6%)
  matrix products  52.6 us (3%)
  other arithmetic  26.5 us (1%)
    unnamed x7, waiting for transfers between devices  1370 us
    all_gather x1, blocking collectives, shards(): all_text = lax.all_gather(text_emb, 'dp', axis=0, tiled=True)  184 us
    all_gather x1, waiting for transfers between devices, shards(): full_images = lax.all_gather(images, 'mp', axis=2, tiled=True)  46.7 us
    concatenate x1, local copies, waits for them, and re-layouts, shards(): jnp.concatenate([first_part, block_part, text_part], axis=1)  38.9 us
  transfers between devices with their start and end apart: 4, of which 3 were waited for; matrix products, arithmetic and copies ran while one was open for 3% of the time, Pallas kernels for 0%

commit v1 on v0

v1 whole, which is shorter than its diff:
```python
import jax
import jax.numpy as jnp
from jax import lax
from jax.sharding import PartitionSpec as P

sqrt_two_pi = 0.7978845608028654
cubic_term = 0.044715
epsilon = 1e-06
HIGHEST = lax.Precision.HIGHEST


def gelu_and_slope(values):
    squared = values * values
    tanh_part = jnp.tanh(sqrt_two_pi * (values + cubic_term * values * squared))
    half = 0.5 * (1.0 + tanh_part)
    slope = half + 0.5 * values * (1.0 - tanh_part * tanh_part) * sqrt_two_pi * (
        1.0 + 3.0 * cubic_term * squared
    )
    return values * half, slope


def layer_norm(image_rows, ln_gain):
    values = image_rows.astype(jnp.float32)
    centered = values - jnp.mean(values, axis=-1, keepdims=True)
    spread = jnp.mean(centered * centered, axis=-1, keepdims=True)
    return (centered * lax.rsqrt(spread + epsilon) * ln_gain).astype(jnp.bfloat16)


def dot(a, b, dims, precision=None):
    return lax.dot_general(
        a, b, (dims, ((), ())), preferred_element_type=jnp.float32, precision=precision
    )


def shards(images, ln_gain, w_in, b_in, w_out, texts, w_text, b_text, logit_scale, logit_bias):
    count, patches, _ = images.shape
    full = lax.all_gather(images, "mp", axis=2, tiled=True)
    texts_all = lax.all_gather(texts, "dp", axis=0, tiled=True)
    width = full.shape[2]
    batch = texts_all.shape[0]
    act_sums, products = [], []
    for i in range(count):
        normed = layer_norm(full[i], ln_gain)
        before = dot(normed, w_in, ((1,), (0,))) + b_in
        act, slope = gelu_and_slope(before)
        act_sums.append(
            jnp.sum(act.astype(jnp.bfloat16), axis=0, keepdims=True, dtype=jnp.float32)
        )
        products.append(dot(normed, slope.astype(jnp.bfloat16), ((0,), (0,))))
    act_sum = jnp.concatenate(act_sums, axis=0)
    block_sum = dot(act_sum, w_out.astype(jnp.float32), ((1,), (0,)), HIGHEST)
    block_sum = lax.psum(block_sum, "mp")
    pooled_own = (jnp.sum(full.astype(jnp.float32), axis=1) + block_sum) / patches
    pooled = lax.all_gather(pooled_own, "dp", axis=0, tiled=True)
    act_sum_all = lax.all_gather(act_sum, "dp", axis=0, tiled=True)

    image_norm = jnp.sqrt(jnp.sum(pooled * pooled, axis=1, keepdims=True) + epsilon)
    image_unit = pooled / image_norm
    image_emb = image_unit.astype(jnp.bfloat16)
    text_proj = dot(texts_all, w_text, ((1,), (0,))) + b_text
    text_norm = jnp.sqrt(jnp.sum(text_proj * text_proj, axis=1, keepdims=True) + epsilon)
    text_unit = text_proj / text_norm
    text_emb = text_unit.astype(jnp.bfloat16)
    logits = logit_scale[0] * dot(image_emb, text_emb, ((1,), (1,))) + logit_bias[0]
    signs = jnp.where(jnp.eye(batch, dtype=bool), 1.0, -1.0)
    scaled = (logit_scale[0] * (-signs * jax.nn.sigmoid(-signs * logits))).astype(jnp.bfloat16)
    grad_image_emb = dot(scaled, text_emb, ((1,), (0,)))
    grad_text_emb = dot(scaled, image_emb, ((0,), (0,)))
    grad_pooled = (
        grad_image_emb - image_unit * jnp.sum(image_unit * grad_image_emb, axis=1, keepdims=True)
    ) / image_norm
    grad_block = (grad_pooled / patches).astype(jnp.bfloat16)
    grad_text_proj = (
        (grad_text_emb - text_unit * jnp.sum(text_unit * grad_text_emb, axis=1, keepdims=True))
        / text_norm
    ).astype(jnp.bfloat16)

    place = lax.axis_index("dp")
    own_block = lax.dynamic_slice_in_dim(grad_block, place * count, count, 0)
    own_text_grad = lax.dynamic_slice_in_dim(grad_text_proj, place * count, count, 0)
    rows = width // lax.axis_size("dp")
    grad_texts = dot(own_text_grad, w_text, ((1,), (1,))).astype(jnp.bfloat16)
    own_features = lax.dynamic_slice_in_dim(texts_all, place * rows, rows, 1)
    grad_w_text = dot(own_features, grad_text_proj, ((0,), (0,)))
    own_columns = lax.dynamic_slice_in_dim(grad_block, place * rows, rows, 1)
    grad_w_out = dot(act_sum_all, own_columns.astype(jnp.float32), ((0,), (0,)), HIGHEST)

    grad_act = dot(own_block, w_out, ((1,), (1,)))
    total = products[0] * grad_act[0:1]
    for i in range(1, count):
        total = total + products[i] * grad_act[i : i + 1]
    grad_w_in = lax.psum_scatter(total, "dp", scatter_dimension=0, tiled=True)
    return (grad_w_in, grad_w_out, grad_w_text, grad_texts)


def solution(mesh):
    placed = (
        P("dp", None, "mp"),
        P(),
        P(None, "mp"),
        P("mp"),
        P("mp", None),
        P("dp", None),
        P(),
        P(),
        P(),
        P(),
    )
    return jax.shard_map(
        shards,
        mesh=mesh,
        in_specs=placed,
        out_specs=(P("dp", "mp"), P("mp", "dp"), P("dp", None), P("dp", None)),
        check_vma=False,
    )
```

time: 1810 us -> 1130 us (0.62)
  waiting for transfers between devices: 1420 us -> 497 us
  blocking collectives: 189 us -> 568 us
  local copies, waits for them, and re-layouts: 106 us -> 8.09 us
  matrix products: 52.6 us -> 31.5 us
  other arithmetic: 26.5 us -> 7.91 us
    unnamed x7 -> x3, waiting for transfers between devices: 1370 us -> 497 us
    all_gather x2 -> x3, blocking collectives: 189 us -> 562 us  [the longest x1 189 us: shards(): act_sum_all = lax.all_gather(act_sum, 'dp', axis=0, tiled=True)]
    all_gather x1, waiting for transfers between devices: 46.7 us -> 0.01 us  [shards(): full = lax.all_gather(images, 'mp', axis=2, tiled=True)]
    concatenate x1 -> x0, local copies, waits for them, and re-layouts: 38.9 us -> none  [shards(): jnp.concatenate([first_part, block_part, text_part], axis=1)]
    convert_element_type x5 -> x0, local copies, waits for them, and re-layouts: 37.3 us -> none  [the longest x2 14.9 us: shards(): partial_out.astype(jnp.bfloat16)]
    dot_general x11 -> x13, matrix products: 52.6 us -> 31.5 us  [dot(): lax.dot_general(a, b, (dims, ((), ())), preferred_element_type=jnp.float3...]
  transfers between devices with their start and end apart: 4 -> 2, of which waited for: 3 -> 1; matrix products, arithmetic and copies ran while one was open for 3% -> 1% of each run, Pallas kernels for 0% -> 0%
where the time goes in v1:
time: 1130 us
  blocking collectives  568 us (50%)
  waiting for transfers between devices  497 us (44%)
  matrix products  31.5 us (3%)
  between operations  16.4 us (1%)
    unnamed x3, waiting for transfers between devices  497 us
    all_gather x1, blocking collectives, shards(): act_sum_all = lax.all_gather(act_sum, 'dp', axis=0, tiled=True)  189 us
    all_gather x1, blocking collectives, shards(): pooled = lax.all_gather(pooled_own, 'dp', axis=0, tiled=True)  187 us
    all_gather x1, blocking collectives, shards(): texts_all = lax.all_gather(texts, 'dp', axis=0, tiled=True)  186 us
    dot_general x13, matrix products, dot(): lax.dot_general(a, b, (dims, ((), ())), preferred_element_type=jnp.float3...  31.5 us
  transfers between devices with their start and end apart: 2, of which 1 were waited for; matrix products, arithmetic and copies ran while one was open for 1% of the time, Pallas kernels for 0%

profile of v1, /device:TPU:8, one launch (start us, length us, event | category | flops | bytes accessed | tf_op | source)
XLA Modules:
  0.0 1129.6 jit_solution(11481539067165697324)
XLA Ops:
  7.2 0.7 all-gather.5.cloned.1.call-update
  9.3 186.0 %all-gather.1 = bf16[64,2,1152]{2,1,0:T(2,128)(2,1)S(1)} all-gather(bf16[1,2,1152]{2,1,0:T(2,128)(2,1)} %bitcast.57), channel_id=1, replica_groups=mesh['dp'=64,'mp'=4] {'dp'}, dimensions={0}, use_global_device_ids=true | all-gather | bytes 299520 | tf_op jit(solution)/shard_map/all_gather | solution.py:38
  195.4 2.1 multiply_reduce_fusion.2
  197.5 0.5 add_sqrt_fusion
  198.0 2.8 convert_reduce_fusion.2
  200.8 0.3 copy-done.1
  201.1 1.0 fusion.4
  202.1 5.0 convert_reduce_fusion.3
  207.2 5.0 convert_reduce_fusion.4
  212.2 1.1 fusion.50
  213.3 5.9 psum.7
  219.2 2.6 convert_reduce_fusion
  221.8 187.1 %all-gather = f32[64,2,1152]{2,1,0:T(2,128)} all-gather(f32[1,2,1152]{2,1,0:T(2,128)S(1)} %multiply_bitcast_fusion), channel_id=1, replica_groups=mesh['dp'=64,'mp'=4] {'dp'}, dimensions={0}, use_global_device_ids=true | all-gather | bytes 599040 | tf_op jit(solution)/shard_map/all_gather | solution.py:54
  409.0 1.5 reshape.52
  410.4 0.1 multiply_reduce_fusion.3
  410.6 1.6 fusion.31
  412.3 1.1 multiply_reduce_fusion.1
  413.4 0.2 multiply_convert_fusion.2
  413.6 0.7 fusion.47
  414.5 0.9 copy-done.23
  415.4 3.3 convolution_multiply_fusion
  418.8 5.7 fusion
  424.5 1.3 dynamic-slice
  426.5 189.2 %all-gather.2 = f32[64,2,1076]{2,1,0:T(2,128)} all-gather(f32[1,2,1076]{2,1,0:T(2,128)S(1)} %fusion.49), channel_id=1, replica_groups=mesh['dp'=64,'mp'=4] {'dp'}, dimensions={0}, use_global_device_ids=true | all-gather | bytes 559520 | tf_op jit(solution)/shard_map/all_gather | solution.py:55
  615.7 2.3 reshape.56
  618.0 1.6 multiply_reduce_fusion
  619.6 0.7 divide_convert_fusion
  620.3 0.9 fusion.42
  621.2 1.9 fusion.44
  623.1 1.4 convolution_convert_fusion
  624.5 496.7 %all-reduce.3.cloned.1.call-done = f32[1152,1076]{1,0:T(8,128)} async-done(((f32[1152,1076]{1,0:T(8,128)}), f32[1152,1076]{1,0:T(8,128)}) %all-reduce.3.cloned.1.call-update) | async-done | bytes 4958224
  1121.2 1.6 constant_dynamic-slice_fusion
  (62 shorter events, 0.4 us)
Async XLA Ops:
  7.2 188.2 %copy-start = (bf16[1152,1152]{1,0:T(8,128)(2,1)S(1)}, bf16[1152,1152]{1,0:T(8,128)(2,1)}, u32[]{:S(2)}) copy-start(bf16[1152,1152]{1,0:T(8,128)(2,1)} %param.16) | copy-start | bytes 7962628
  7.2 190.8 %all-gather.5.cloned.1.call-start = ((), (), s32[]{:S(2)}) async-start(), calls=%async_computation | async-start | bytes 4423680 | tf_op jit(solution)/shard_map/all_gather | solution.py:37
  7.9 1113.3 %all-reduce.3.cloned.1.call-start = ((), (), s32[]{:S(2)}) async-start(), calls=%async_computation.1 | async-start | bytes 10616832
  198.0 4.1 copy-start.19
  198.0 4.1 copy-start.20
  198.0 3.1 copy-start.1
  198.0 4.1 copy-start.18
  200.8 6.4 copy-start.11
  200.8 6.4 copy-start.9
  202.1 5.1 copy-start.13
  202.1 5.0 copy-start.15
  207.2 5.1 copy-start.3
  410.4 1.7 copy-start.6
  410.6 2.8 copy-start.17
  410.6 3.0 copy-start.4
  412.2 1.2 copy-start.24
  412.2 2.2 copy-start.2
  412.2 2.2 copy-start.12
  412.2 2.2 copy-start.16
  412.2 2.2 copy-start.21
  412.2 3.2 copy-start.23
  413.6 0.8 copy-start.8
  415.4 3.3 copy-start.10
  415.4 3.3 copy-start.14
  415.4 3.3 copy-start.22
  617.9 1.6 copy-start.7
  618.0 3.3 copy-start.5
Sparse Core Ops, SparseCore 0:
  9.8 45.5 all-gather.4
  424.6 696.5 all-reduce.2

commit v2 on v1

v2 whole, which is shorter than its diff:
```python
import jax
import jax.numpy as jnp
from jax import lax
from jax.experimental import pallas as pl
from jax.experimental.pallas import tpu as pltpu
from jax.sharding import PartitionSpec as P

sqrt_two_pi = 0.7978845608028654
cubic_term = 0.044715
epsilon = 1e-06

NX, NH, NZ, NM = 4, 2, 8, 4
D = 1152
HID = 1076
PATCH = 729
OWN = D // 4
TILE = 256
TILES = 3
ROWS = 18
PAIR = 48
GROUPS_A = ((0, 640),)
GROUPS_B = ((640, 512),)
AHEAD = 3
PADDED = 1088
BATCH = 128
HALF = 64

f32 = jnp.float32
b16 = jnp.bfloat16
MESH = pl.DeviceIdType.MESH


def mm(a, b):
    return lax.dot_general(a, b, (((1,), (0,)), ((), ())), preferred_element_type=f32)


def mm_nt(a, b):
    return lax.dot_general(a, b, (((1,), (1,)), ((), ())), preferred_element_type=f32)


def mm_tn(a, b):
    return lax.dot_general(a, b, (((0,), (0,)), ((), ())), preferred_element_type=f32)


class Refs:
    def __init__(self, values):
        for name, value in values.items():
            setattr(self, name, Refs(value) if isinstance(value, dict) else value)


def iota(shape, axis):
    return lax.broadcasted_iota(jnp.int32, shape, axis)


def three_parts(values):
    high = values.astype(b16)
    rest = values - high.astype(f32)
    middle = rest.astype(b16)
    low = (rest - middle.astype(f32)).astype(b16)
    return high, middle, low


def gelu_and_slope(values):
    squared = values * values
    tanh_part = jnp.tanh(values * (sqrt_two_pi + (sqrt_two_pi * cubic_term) * squared))
    half = 0.5 + 0.5 * tanh_part
    bend = (1.0 - tanh_part * tanh_part) * (
        0.5 * sqrt_two_pi + (1.5 * sqrt_two_pi * cubic_term) * squared
    )
    return values * half, half + values * bend


def kernel(
    images,
    gain_row,
    bias_in,
    bias_text,
    texts,
    scale_ref,
    shift_ref,
    w_in_hbm,
    w_out_hbm,
    w_text_hbm,
    out_in,
    out_out,
    out_text,
    out_texts,
    s,
):
    s = Refs(s)
    w_in, w_tail, w_out, w_text = s.w_in, s.w_tail, s.w_out, s.w_text
    full, normed, slopes, product = s.full, s.normed, s.slopes, s.product
    act_sum, image_sum, grad_act, parts = s.act_sum, s.image_sum, s.grad_act, s.parts

    dp = lax.axis_index("dp")
    mp = lax.axis_index("mp")
    x = dp // (NH * NZ)
    yh = (dp // NZ) % NH
    z = dp % NZ
    slot = yh * (NX * NZ) + x * NZ + z
    yl = mp // 2
    core = mp % 2
    mp_chip = (1 - yl) * 2 + core
    mp_core = yl * 2 + (1 - core)
    mp_far = (1 - yl) * 2 + (1 - core)
    chip, other, far = (dp, mp_chip), (dp, mp_core), (dp, mp_far)

    def at_z(d):
        return ((x * NH + yh) * NZ + (z + d) % NZ, mp)

    def at_x(d):
        return ((((x + d) % NX) * NH + yh) * NZ + z, mp)

    def at_yh():
        return ((x * NH + (1 - yh)) * NZ + z, mp)

    def remote(src, dst, send_sem, recv_sem, device):
        return pltpu.make_async_remote_copy(
            src_ref=src,
            dst_ref=dst,
            send_sem=send_sem,
            recv_sem=recv_sem,
            device_id=device,
            device_id_type=MESH,
        )

    sent = []

    def send(src, dst, send_sem, recv_sem, device):
        copy = remote(src, dst, send_sem, recv_sem, device)
        copy.start()
        sent.append(copy)

    def arrived(dst, send_sem, recv_sem, device):
        remote(dst, dst, send_sem, recv_sem, device).wait_recv()

    loads = [
        pltpu.make_async_copy(w_in_hbm, w_in, s.load_sem.at[0]),
        pltpu.make_async_copy(w_out_hbm, w_out, s.load_sem.at[1]),
        pltpu.make_async_copy(w_text_hbm, w_text, s.load_sem.at[2]),
    ]
    for load in loads:
        load.start()

    barrier = pltpu.get_barrier_semaphore()
    partners = [chip, other, far, at_yh()]
    partners += [at_z(d) for d in range(1, NZ)] + [at_x(d) for d in range(1, NX)]
    for partner in partners:
        pl.semaphore_signal(barrier, inc=1, device_id=partner, device_id_type=MESH)

    for i in range(2):
        for j in range(TILES):
            begin = j * TILE
            width = min(TILE, PATCH - begin)
            if width < TILE:
                full[i * TILES + j, mp] = jnp.zeros((OWN, TILE), b16)
            full[i * TILES + j, mp, :, 0:width] = images[i, :, begin : begin + width]
    s.texts.buf[yh, x, z] = texts[...].astype(f32)

    pl.semaphore_wait(barrier, len(partners))

    class Gather:
        def __init__(self, refs):
            self.buf, self.send_sem, self.recv_sem = refs.buf, refs.send, refs.recv

        def copies(self, stage):
            if stage == 0:
                return [
                    (d, self.buf.at[yh, x, z], self.buf.at[yh, x, (z + NZ - d) % NZ], at_z(d))
                    for d in range(1, NZ)
                ]
            if stage == 1:
                return [
                    (7 + d, self.buf.at[yh, x], self.buf.at[yh, (x + NX - d) % NX], at_x(d))
                    for d in range(1, NX)
                ]
            return [(0, self.buf.at[yh], self.buf.at[1 - yh], at_yh())]

        def start(self, stage):
            for n, own, _, device in self.copies(stage):
                remote(own, own, self.send_sem.at[n], self.recv_sem.at[n], device).start()

        def wait(self, stage):
            for n, _, landed, device in self.copies(stage):
                arrived(landed, self.send_sem.at[n], self.recv_sem.at[n], device)

        def drain(self):
            for stage in range(3):
                for n, own, _, device in self.copies(stage):
                    remote(own, own, self.send_sem.at[n], self.recv_sem.at[n], device).wait_send()

    def tile_copy(k, t):
        source = full.at[t, mp_chip if k == 2 else mp]
        return remote(source, source, s.img.send.at[k, t], s.img.recv.at[k, t], chip if k == 0 else other)

    text_gather = Gather(s.texts)
    for t in range(AHEAD):
        tile_copy(0, t).start()
        tile_copy(1, t).start()
    text_gather.start(0)

    product[...] = jnp.zeros_like(product)
    act_sum[...] = jnp.zeros_like(act_sum)
    image_sum[...] = jnp.zeros_like(image_sum)
    grad_act[...] = jnp.zeros_like(grad_act)
    diagonal = iota((128, 128), 0) == iota((128, 128), 1)
    row_pad = s.row_pad
    for row, column, width in ((gain_row, s.gain_col, D), (bias_in, s.bias_col, HID)):
        row_pad[...] = jnp.zeros_like(row_pad)
        row_pad[:, 0:width] = row[...].reshape(1, width)
        for k in range(D // 128):
            span = slice(128 * k, 128 * k + 128)
            picked = jnp.sum(jnp.where(diagonal, row_pad[:, span], 0.0), axis=1, keepdims=True)
            column[span, :] = jnp.broadcast_to(picked, (128, 128))
    whole = HID // TILE * TILE
    chunks = [(begin, TILE) for begin in range(0, whole, TILE)] + [(whole, PADDED - whole)]
    loads[0].wait()
    tail = (iota((PADDED - whole, HID - whole), 0) == iota((PADDED - whole, HID - whole), 1)).astype(
        b16
    )
    w_tail[...] = mm(tail, w_in[whole:HID, :]).astype(b16)

    def add_product(t):
        i = t // TILES
        for begin, width in chunks:
            span = slice(begin, begin + width)
            product[i, :, span] += mm_nt(normed[t], slopes[t, span, :])

    def work_on(t):
        i = t // TILES
        j = t % TILES
        for h in range(TILE // 128):
            lanes = slice(128 * h, 128 * h + 128)
            total = jnp.zeros((1, 128), f32)
            for m in range(NM):
                total += jnp.sum(full[t, m, :, lanes].astype(f32), axis=0, keepdims=True)
            mean = total * (1.0 / D)
            total = jnp.zeros((1, 128), f32)
            for m in range(NM):
                centered = full[t, m, :, lanes].astype(f32) - mean
                total += jnp.sum(centered * centered, axis=0, keepdims=True)
            factor = lax.rsqrt(total * (1.0 / D) + epsilon)
            for m in range(NM):
                rows = slice(OWN * m, OWN * m + OWN)
                centered = full[t, m, :, lanes].astype(f32) - mean
                normed[t, rows, lanes] = (centered * factor * s.gain_col[rows, :]).astype(b16)
        valid = (iota((8, TILE), 1) + j * TILE < PATCH).astype(b16)
        image_sum[i] += mm_nt(valid, full[t].reshape(D, TILE))
        for begin, width in chunks:
            span = slice(begin, begin + width)
            bias = s.bias_col[span, :]
            weight = w_in[span, :] if begin < whole else w_tail[...]
            before = mm(weight, normed[t]) + jnp.concatenate([bias, bias], axis=1)
            act, slope = gelu_and_slope(before)
            slopes[t, span, :] = slope.astype(b16)
            act_sum[i, :, span] += mm_nt(valid, act.astype(b16))

    def project_texts():
        loads[2].wait()
        for r in range(2):
            s.text_rows[HALF * r : HALF * r + HALF, :] = (
                s.texts.buf[:, :, :, r, :].reshape(HALF, D).astype(b16)
            )
        projected = mm(s.text_rows[...], w_text[...]) + bias_text[...].reshape(1, D)
        norm = jnp.sqrt(jnp.sum(projected * projected, axis=1, keepdims=True) + epsilon)
        unit = projected / norm
        s.text_norm[...] = jnp.broadcast_to(norm, (BATCH, 128))
        s.text_unit[...] = unit
        s.text_emb[...] = unit.astype(b16)

    def tile_step(t, carry):
        arrived(full.at[t, mp_chip], s.img.send.at[0, t], s.img.recv.at[0, t], chip)
        tile_copy(2, t).start()

        @pl.when(t < 2 * TILES - AHEAD)
        def _():
            tile_copy(0, t + AHEAD).start()
            tile_copy(1, t + AHEAD).start()

        @pl.when(t > 0)
        def _():
            add_product(t - 1)

        @pl.when(t == 1)
        def _():
            text_gather.wait(0)
            text_gather.start(1)

        @pl.when(t == 3)
        def _():
            text_gather.wait(1)
            text_gather.start(2)

        @pl.when(t == 5)
        def _():
            text_gather.wait(2)
            project_texts()

        arrived(full.at[t, mp_core], s.img.send.at[1, t], s.img.recv.at[1, t], other)
        arrived(full.at[t, mp_far], s.img.send.at[2, t], s.img.recv.at[2, t], other)
        work_on(t)
        return carry

    lax.fori_loop(0, 2 * TILES, tile_step, 0)

    loads[1].wait()
    row = iota((8, HID), 0)
    split = three_parts(act_sum[0, :, 0:HID]) + three_parts(act_sum[1, :, 0:HID])
    stacked = jnp.zeros((8, HID), f32)
    for k in range(6):
        stacked = jnp.where(row == k, split[k].astype(f32), stacked)
    shares = mm(stacked.astype(b16), w_out[...])
    row = iota((8, D), 0)
    share_0 = jnp.sum(jnp.where(row < 3, shares, 0.0), axis=0, keepdims=True)
    share_1 = jnp.sum(jnp.where((row >= 3) & (row < 6), shares, 0.0), axis=0, keepdims=True)
    first = iota((2, D), 0) == 0
    parts[mp] = jnp.where(first, share_0, share_1)
    group = (chip, other, far)
    for k, partner in enumerate(group):
        own = parts.at[mp]
        send(own, own, s.part.send.at[k], s.part.recv.at[k], partner)
    add_product(2 * TILES - 1)
    for k, source in enumerate((mp_chip, mp_core, mp_far)):
        arrived(parts.at[source], s.part.send.at[k], s.part.recv.at[k], group[k])
    block = parts[0] + parts[1] + parts[2] + parts[3]
    pooled = (jnp.where(first, image_sum[0, 0:2, :], image_sum[1, 0:2, :]) + block) * (1.0 / PATCH)
    pool_gather = Gather(s.pool)
    mine = jnp.where(core == 0, pooled[0:1, :], pooled[1:2, :])
    pooled_high = mine.astype(b16)
    pooled_rest = (mine - pooled_high.astype(f32)).astype(b16)
    rows = (pooled_high.astype(f32), pooled_rest.astype(f32), act_sum[0, 0:1, :], act_sum[1, 0:1, :])
    order = iota((4, D), 0)
    packed = jnp.broadcast_to(rows[0], (4, D))
    for k in range(1, 4):
        packed = jnp.where(order == k, rows[k], packed)
    s.pool.buf[yh, x, z] = packed.astype(b16)
    pool_gather.start(0)

    scale = scale_ref[0]
    shift = shift_ref[0]

    def block_gradient(values):
        norm = jnp.sqrt(jnp.sum(values * values, axis=1, keepdims=True) + epsilon)
        unit = values / norm
        emb = unit.astype(b16)
        logits = scale * mm_nt(emb, s.text_emb[...]) + shift
        if values.shape[0] == 2:
            matches = iota((2, BATCH), 1) == iota((2, BATCH), 0) * HALF + slot
        else:
            matches = iota((BATCH, BATCH), 0) == iota((BATCH, BATCH), 1)
        signs = jnp.where(matches, 1.0, -1.0)
        coef = -signs * jax.nn.sigmoid(-signs * logits)
        weights = (scale * coef).astype(b16)
        grad_emb = mm(weights, s.text_emb[...])
        along = jnp.sum(unit * grad_emb, axis=1, keepdims=True)
        grad_pooled = (grad_emb - unit * along) / norm
        return (grad_pooled * (1.0 / PATCH)).astype(b16), weights, emb

    own_block, _, _ = block_gradient(pooled)
    grad_act[:, 0:HID] = mm_nt(own_block, w_out[...])

    near_z = (at_z(1), at_z(NZ - 1))
    near_x = (at_x(1), at_x(NX - 1))

    def add_into(target, index, begin, count, received):
        for r in range(0, count, 48):
            there = slice(begin + r, begin + r + 48)
            target[index, there, :] = (
                target[index, there, :].astype(f32) + received[r : r + 48, :].astype(f32)
            ).astype(b16)

    class Ring:
        def __init__(self, refs, place, size, near, steps):
            self.buf = refs.buf
            self.recv = refs.right, refs.left
            self.sems = refs.send, refs.recv
            self.place, self.size, self.near, self.steps = place, size, near, steps

        def wait(self, way, k):
            n = way * self.steps[0] + k - 1
            there = self.recv[way].at[k - 1]
            arrived(there, self.sems[0].at[n], self.sems[1].at[n], self.near[way])
            return there

        def step(self, k):
            for way in range(2):
                if k > self.steps[way]:
                    continue
                away = self.steps[way] + 1 - k
                chunk = (self.place + (self.size - away if way else away)) % self.size
                if k > 1:
                    add_into(self.buf, chunk, 0, self.buf.shape[1], self.wait(way, k - 1))
                n = way * self.steps[0] + k - 1
                send(
                    self.buf.at[chunk],
                    self.recv[way].at[k - 1],
                    self.sems[0].at[n],
                    self.sems[1].at[n],
                    self.near[way],
                )

        def finish(self):
            for way in range(2):
                self.wait(way, self.steps[way])

        def total(self, rows):
            value = self.buf[self.place, rows, :].astype(f32)
            for way in range(2):
                value += self.recv[way][self.steps[way] - 1, rows, :].astype(f32)
            return value

    class Group:
        def __init__(self, refs, begin, width):
            self.refs, self.begin, self.width = refs, begin, width
            self.span = slice(begin, begin + width)

        def send_pair(self, ring):
            ring.finish()
            value = ring.total(slice(0, PAIR))
            for h in range(NH):
                self.refs.pair.buf[h] = value[24 * h : 24 * h + 24, :]
            sems = self.refs.pair.send.at[0], self.refs.pair.recv.at[0]
            send(self.refs.pair.buf.at[1 - yh], self.refs.pair.right, *sems, at_yh())

        def result(self):
            sems = self.refs.pair.send.at[0], self.refs.pair.recv.at[0]
            arrived(self.refs.pair.right, *sems, at_yh())
            width = min(self.width, HID - self.begin)
            value = self.refs.pair.buf[yh] + self.refs.pair.right[...]
            out_in[:, self.begin : self.begin + width] = value[0:ROWS, 0:width]

    class GroupA(Group):
        def __init__(self, refs, begin, width, steps):
            super().__init__(refs, begin, width)
            self.z = Ring(refs.ring, z, NZ, near_z, steps)
            self.q1, self.q2, self.q3 = (x + 1) % NX, (x + 2) % NX, (x + 3) % NX

        def combine(self, q):
            for r in range(OWN // 48):
                rows = pl.ds(pl.multiple_of(q * OWN + 48 * r, 16), 48)
                self.refs.stage.buf[q, 48 * r : 48 * r + 48, :] = (
                    product[0, rows, self.span] * grad_act[0:1, self.span]
                    + product[1, rows, self.span] * grad_act[1:2, self.span]
                ).astype(b16)

        def pieces(self, way, k):
            n = way * 3 + k
            return (
                (self.refs.stage.left if way else self.refs.stage.right).at[k],
                self.refs.stage.send.at[n],
                self.refs.stage.recv.at[n],
                near_x[way],
            )

        def send_half(self, q, half, way, k):
            send(self.refs.stage.buf.at[q, pl.ds(144 * half, 144)], *self.pieces(way, k))

        def wait_half(self, way, k):
            arrived(*self.pieces(way, k))

        def first(self):
            self.combine(self.q2)
            self.send_half(self.q2, 0, 0, 0)
            self.send_half(self.q2, 1, 1, 0)

        def second(self):
            self.combine(self.q1)
            self.send_half(self.q1, 1, 0, 1)
            self.combine(self.q3)
            self.send_half(self.q3, 0, 1, 1)

        def third(self):
            self.wait_half(0, 0)
            add_into(self.refs.stage.buf, self.q1, 0, 144, self.refs.stage.right.at[0])
            self.send_half(self.q1, 0, 0, 2)
            self.wait_half(1, 0)
            add_into(self.refs.stage.buf, self.q3, 144, 144, self.refs.stage.left.at[0])
            self.send_half(self.q3, 1, 1, 2)

        def finish_x(self):
            total = self.refs.sum
            for k in range(1, 3):
                self.wait_half(0, k)
                self.wait_half(1, k)
            for half in range(2):
                for r in range(0, 144, 48):
                    there = slice(144 * half + r, 144 * half + r + 48)
                    here = slice(r, r + 48)
                    total[there, :] = (
                        self.refs.stage.buf[x, there, :].astype(f32)
                        + self.refs.stage.right[2 - half, here, :].astype(f32)
                        + self.refs.stage.left[1 + half, here, :].astype(f32)
                    )
            total[OWN : OWN + 8, :] = jnp.zeros((8, self.width), f32)
            for k in range(NZ):
                both = [
                    total[h * (NZ * ROWS) + k * ROWS : h * (NZ * ROWS) + k * ROWS + 24, :]
                    for h in range(NH)
                ]
                self.refs.ring.buf[k] = jnp.concatenate(both, axis=0).astype(b16)

    class GroupB(Group):
        def __init__(self, refs, begin, width, steps):
            super().__init__(refs, begin, width)
            self.z = Ring(refs.stage, z, NZ, near_z, steps)
            self.x = Ring(refs.ring, x, NX, near_x, (2, 1) if steps[0] > steps[1] else (1, 2))

        def pack(self):
            pack = self.refs.pack
            weight_0, weight_1 = grad_act[0:1, self.span], grad_act[1:2, self.span]
            for k in range(NZ):
                for g in range(NX * NH):
                    begin = g * (NZ * ROWS) + k * ROWS
                    source = slice(begin, begin + ROWS)
                    pack[g * ROWS : g * ROWS + ROWS, :] = (
                        product[0, source, self.span] * weight_0
                        + product[1, source, self.span] * weight_1
                    )
                self.refs.stage.buf[k] = pack[...].astype(b16)

        def finish_z(self):
            self.z.finish()
            total = self.refs.sum
            for r in range(0, 144, 48):
                total[r : r + 48, :] = self.z.total(slice(r, r + 48))
            total[144:152, :] = jnp.zeros((8, self.width), f32)
            for k in range(NX):
                both = [
                    total[(k * NH + h) * ROWS : (k * NH + h) * ROWS + 24, :] for h in range(NH)
                ]
                self.refs.ring.buf[k] = jnp.concatenate(both, axis=0).astype(b16)

    a = GroupA(s.a, *GROUPS_A[0], (3, 4))
    b = GroupB(s.b, *GROUPS_B[0], (4, 3))

    pairs = Refs({})

    def pairs_1():
        halves = []
        for buf in (s.pool.buf, s.pool_other):
            both = [buf[:, :, :, r, :].reshape(HALF, D).astype(f32) for r in range(2)]
            halves.append(both[0] + both[1])
        lower = jnp.where(core == 0, halves[0], halves[1])
        upper = jnp.where(core == 0, halves[1], halves[0])
        all_pooled = jnp.concatenate([lower, upper], axis=0)
        block, weights, emb = block_gradient(all_pooled)
        pick = (iota((D, ROWS), 0) == iota((D, ROWS), 1) + dp * ROWS).astype(b16)
        pairs.columns = mm(block, pick).astype(b16)
        pairs.features = mm(s.text_rows[...], pick).astype(b16)
        pairs.weights, pairs.emb = weights, emb

    def pairs_2():
        grad_text = mm_tn(pairs.weights, pairs.emb)
        unit = s.text_unit[...]
        along = jnp.sum(unit * grad_text, axis=1, keepdims=True)
        pairs.proj = ((grad_text - unit * along) / s.text_norm[:, 0:1]).astype(b16)

    def pairs_3():
        acts = jnp.concatenate(
            [s.pool.buf[:, :, :, 2 + r, 0:HID].reshape(HALF, HID) for r in range(2)], axis=0
        )
        out_out[...] = mm_tn(pairs.columns, acts)

    def pairs_4():
        out_text[...] = mm_tn(pairs.features, pairs.proj)
        chosen = (iota((2, BATCH), 1) == iota((2, BATCH), 0) * HALF + slot).astype(b16)
        own_text = mm(chosen, pairs.proj).astype(b16)
        out_texts[...] = mm_nt(own_text, w_text[...]).astype(b16)

    a.first()
    b.pack()
    b.z.step(1)
    a.second()
    pool_gather.wait(0)
    pool_gather.start(1)
    a.third()
    b.z.step(2)
    a.combine(x)
    b.z.step(3)
    pool_gather.wait(1)
    pool_gather.start(2)
    a.finish_x()
    a.z.step(1)
    b.z.step(4)
    a.z.step(2)
    b.finish_z()
    b.x.step(1)
    a.z.step(3)
    pool_gather.wait(2)
    core_sems = s.core.send.at[0], s.core.recv.at[0]
    send(s.pool.buf, s.pool_other, *core_sems, other)
    b.x.step(2)
    a.z.step(4)
    arrived(s.pool_other, *core_sems, other)
    pairs_1()
    b.send_pair(b.x)
    pairs_2()
    a.send_pair(a.z)
    pairs_3()
    pairs_4()
    b.result()
    a.result()
    for copy in sent:
        copy.wait_send()
    for gather in (text_gather, pool_gather):
        gather.drain()

    def drain_tiles(t, carry):
        for k in range(3):
            tile_copy(k, t).wait_send()
        return carry

    lax.fori_loop(0, 2 * TILES, drain_tiles, 0)


def hand_on(*refs):
    sems = refs[8]
    copies = [pltpu.make_async_copy(refs[k], refs[4 + k], sems.at[k]) for k in range(4)]
    for copy in copies:
        copy.start()
    for copy in copies:
        copy.wait()


def shards(images, ln_gain, w_in, b_in, w_out, texts, w_text, b_text, logit_scale, logit_bias):
    vmem = pl.BlockSpec(memory_space=pltpu.VMEM)
    smem = pl.BlockSpec(memory_space=pltpu.SMEM)
    hbm = pl.BlockSpec(memory_space=pl.ANY)
    dma = pltpu.SemaphoreType.DMA
    V = pltpu.VMEM
    def with_sems(count, **buffers):
        return dict(send=dma(count), recv=dma(count), **buffers)

    def ring(kind, shape, steps, width):
        return with_sems(
            (sum(steps),),
            buf=V(shape + (width,), kind),
            right=V((steps[0],) + shape[1:] + (width,), kind),
            left=V((steps[1],) + shape[1:] + (width,), kind),
        )

    def pair(width):
        return with_sems((1,), buf=V((NH, 24, width), f32), right=V((24, width), f32))

    refs = dict(
        w_in=V((HID, D), b16),
        w_tail=V((PADDED - HID // TILE * TILE, D), b16),
        w_out=V((HID, D), b16),
        w_text=V((D, D), b16),
        gain_col=V((D, 128), f32),
        bias_col=V((D, 128), f32),
        row_pad=V((1, D), f32),
        full=V((2 * TILES, NM, OWN, TILE), b16),
        normed=V((2 * TILES, D, TILE), b16),
        slopes=V((2 * TILES, PADDED, TILE), b16),
        act_sum=V((2, 8, D), f32),
        image_sum=V((2, 8, D), f32),
        product=V((2, D, D), f32),
        parts=V((NM, 2, D), f32),
        pool_other=V((NH, NX, NZ, 4, D), b16),
        text_rows=V((BATCH, D), b16),
        text_emb=V((BATCH, D), b16),
        text_unit=V((BATCH, D), f32),
        text_norm=V((BATCH, 128), f32),
        grad_act=V((2, D), f32),
        load_sem=dma((3,)),
        img=with_sems((3, 2 * TILES)),
        part=with_sems((3,)),
        core=with_sems((1,)),
        texts=with_sems((11,), buf=V((NH, NX, NZ, 2, D), f32)),
        pool=with_sems((11,), buf=V((NH, NX, NZ, 4, D), b16)),
    )
    width = GROUPS_A[0][1]
    stage = with_sems(
        (6,),
        buf=V((NX, OWN, width), b16),
        right=V((3, 144, width), b16),
        left=V((3, 144, width), b16),
    )
    refs.update(
        a=dict(
            stage=stage,
            sum=V((OWN + 8, width), f32),
            ring=ring(b16, (NZ, PAIR), (3, 4), width),
            pair=pair(width),
        )
    )
    width = GROUPS_B[0][1]
    refs.update(
        b=dict(
            pack=V((144, width), f32),
            stage=ring(b16, (NZ, 144), (4, 3), width),
            sum=V((152, width), f32),
            ring=ring(b16, (NX, PAIR), (2, 1), width),
            pair=pair(width),
        )
    )
    out_shape = [
        jax.ShapeDtypeStruct((ROWS, HID), f32),
        jax.ShapeDtypeStruct((ROWS, HID), f32),
        jax.ShapeDtypeStruct((ROWS, D), f32),
        jax.ShapeDtypeStruct((2, D), b16),
    ]
    results = pl.pallas_call(
        kernel,
        out_shape=out_shape,
        in_specs=[vmem] * 5 + [smem] * 2 + [hbm] * 3,
        out_specs=[vmem] * 4,
        scratch_shapes=[refs],
        compiler_params=pltpu.CompilerParams(
            collective_id=0, has_side_effects=True, vmem_limit_bytes=58 << 20
        ),
    )(
        images.transpose(0, 2, 1),
        ln_gain,
        b_in,
        b_text,
        texts,
        logit_scale,
        logit_bias,
        w_in.T,
        w_out,
        w_text,
    )
    grad_in, grad_out, grad_text, grad_texts = pl.pallas_call(
        hand_on,
        out_shape=out_shape,
        in_specs=[hbm] * 4,
        out_specs=[hbm] * 4,
        scratch_shapes=[dma((4,))],
        compiler_params=pltpu.CompilerParams(vmem_limit_bytes=58 << 20),
    )(*results)
    return grad_in, grad_out.T, grad_text, grad_texts


def solution(mesh):
    placed = (
        P("dp", None, "mp"),
        P(),
        P(None, "mp"),
        P("mp"),
        P("mp", None),
        P("dp", None),
        P(),
        P(),
        P(),
        P(),
    )
    return jax.shard_map(
        shards,
        mesh=mesh,
        in_specs=placed,
        out_specs=(P("dp", "mp"), P("mp", "dp"), P("dp", None), P("dp", None)),
        check_vma=False,
    )
```

time: 1130 us -> 99 us (0.09)
  blocking collectives: 568 us -> 0 us
  waiting for transfers between devices: 497 us -> 0 us
  Pallas kernels: 0 us -> 95.7 us
  matrix products: 31.5 us -> 0 us
  between operations: 16.4 us -> 1.93 us
    all_gather x3 -> x0, blocking collectives: 562 us -> none  [the longest x1 189 us: shards(): act_sum_all = lax.all_gather(act_sum, 'dp', axis=0, tiled=True)]
    unnamed x3 -> x0, waiting for transfers between devices: 497 us -> none
    pallas_call x0 -> x2, Pallas kernels: none -> 95.7 us  [the longest x1 84.3 us: shards(): pl.pallas_call(kernel, out_shape=out_shape, in_specs=[vmem] * 5 + [smem]...]
    dot_general x13 -> x0, matrix products: 31.5 us -> none  [dot(): lax.dot_general(a, b, (dims, ((), ())), preferred_element_type=jnp.float3...]
  transfers between devices with their start and end apart: 2 -> 0, of which waited for: 1 -> 0; matrix products, arithmetic and copies ran while one was open for 1% -> 0% of each run, Pallas kernels for 0% -> 0%
where the time goes in v2:
time: 99 us; the launch traced here: 97.6 us
  Pallas kernels  95.7 us (97%)
  between operations  1.93 us (2%)
    pallas_call x1, Pallas kernels, shards(): pl.pallas_call(kernel, out_shape=out_shape, in_specs=[vmem] * 5 + [smem]...  84.3 us
    pallas_call x1, Pallas kernels, shards(): pl.pallas_call(hand_on, out_shape=out_shape, in_specs=[hbm] * 4, out_spec...  11.3 us

profile of v2, /device:TPU:8, one launch (start us, length us, event | category | flops | bytes accessed | tf_op | source)
XLA Modules:
  0.0 97.6 jit_solution(13810214721615041376)
XLA Ops:
  1.9 84.3 %shard_map.129 = (f32[18,1076]{1,0:T(8,128)}, f32[18,1076]{1,0:T(8,128)}, f32[18,1152]{1,0:T(8,128)}, bf16[2,1152]{1,0:T(2,128)(2,1)}) custom-call(bf16[2,288,729]{2,1,0:T(8,128)(2,1)} %bitcast.4, f32[1152]{0:T(1024)} %gain_row.1, f32[1076]{0:T(1024)} %bias_in.1, f32[1152]{0:T(1024)} %bias_text.1, bf16[2,1152]{1,0:T(2,128)(2,1)} %texts.1, ...), custom_call_target="tpu_custom_call" | custom-call | tf_op jit(solution)/shard_map/pallas_call | solution.py:704
  86.3 11.3 %shard_map.130 = (f32[18,1076]{1,0:T(8,128)}, f32[18,1076]{1,0:T(8,128)}, f32[18,1152]{1,0:T(8,128)}, bf16[2,1152]{1,0:T(2,128)(2,1)}) custom-call(f32[18,1076]{1,0:T(8,128)} %get-tuple-element.12.refs_0_, f32[18,1076]{1,0:T(8,128)} %get-tuple-element.13.refs_1_, f32[18,1152]{1,0:T(8,128)} %get-tuple-element.14.refs_2_, ...), custom_call_target="tpu_custom_call" | custom-call | tf_op jit(solution)/shard_map/pallas_call | solution.py:725

commit v3 on v2

--- a/solution.py
+++ b/solution.py
@@ -18,8 +18,8 @@
 TILES = 3
 ROWS = 18
 PAIR = 48
-GROUPS_A = ((0, 640),)
-GROUPS_B = ((640, 512),)
+GROUPS_A = ((0, 384), (384, 256))
+GROUPS_B = ((640, 256), (896, 256))
 AHEAD = 3
 PADDED = 1088
 BATCH = 128
@@ -45,6 +45,8 @@
 class Refs:
     def __init__(self, values):
         for name, value in values.items():
+            if isinstance(value, (tuple, list)):
+                value = [Refs(part) for part in value]
             setattr(self, name, Refs(value) if isinstance(value, dict) else value)
 
 
@@ -97,7 +99,7 @@
     x = dp // (NH * NZ)
     yh = (dp // NZ) % NH
     z = dp % NZ
-    slot = yh * (NX * NZ) + x * NZ + z
+    slot = (x * NZ + z) * NH + yh
     yl = mp // 2
     core = mp % 2
     mp_chip = (1 - yl) * 2 + core
@@ -155,7 +157,7 @@
             if width < TILE:
                 full[i * TILES + j, mp] = jnp.zeros((OWN, TILE), b16)
             full[i * TILES + j, mp, :, 0:width] = images[i, :, begin : begin + width]
-    s.texts.buf[yh, x, z] = texts[...].astype(f32)
+    s.texts.buf[x, z, yh] = texts[...].astype(f32)
 
     pl.semaphore_wait(barrier, len(partners))
 
@@ -163,19 +165,6 @@
         def __init__(self, refs):
             self.buf, self.send_sem, self.recv_sem = refs.buf, refs.send, refs.recv
 
-        def copies(self, stage):
-            if stage == 0:
-                return [
-                    (d, self.buf.at[yh, x, z], self.buf.at[yh, x, (z + NZ - d) % NZ], at_z(d))
-                    for d in range(1, NZ)
-                ]
-            if stage == 1:
-                return [
-                    (7 + d, self.buf.at[yh, x], self.buf.at[yh, (x + NX - d) % NX], at_x(d))
-                    for d in range(1, NX)
-                ]
-            return [(0, self.buf.at[yh], self.buf.at[1 - yh], at_yh())]
-
         def start(self, stage):
             for n, own, _, device in self.copies(stage):
                 remote(own, own, self.send_sem.at[n], self.recv_sem.at[n], device).start()
@@ -184,16 +173,43 @@
             for n, _, landed, device in self.copies(stage):
                 arrived(landed, self.send_sem.at[n], self.recv_sem.at[n], device)
 
-        def drain(self):
-            for stage in range(3):
+        def drain(self, stages):
+            for stage in range(stages):
                 for n, own, _, device in self.copies(stage):
                     remote(own, own, self.send_sem.at[n], self.recv_sem.at[n], device).wait_send()
+
+    class TextGather(Gather):
+        def copies(self, stage):
+            at = self.buf.at
+            if stage == 0:
+                return [(0, at[x, z, yh], at[x, z, 1 - yh], at_yh())]
+            if stage == 1:
+                return [(d, at[x, z], at[x, (z + NZ - d) % NZ], at_z(d)) for d in range(1, NZ)]
+            return [(7 + d, at[x], at[(x + NX - d) % NX], at_x(d)) for d in range(1, NX)]
+
+    class PoolGather(Gather):
+        def copies(self, stage):
+            at = self.buf.at
+            if stage == 0:
+                return [
+                    (d, at[x, yh, z], at[x, yh, (z + NZ - d) % NZ], at_z(d)) for d in range(1, NZ)
+                ]
+            if stage == 1:
+                return [(0, at[x, yh], at[x, 1 - yh], at_yh())]
+            before, after = (x + NX - 1) % NX, (x + 1) % NX
+            if stage == 2:
+                return [(8, at[x], at[before], at_x(1)), (9, at[x], at[after], at_x(NX - 1))]
+            far = (x + 2) % NX
+            return [
+                (10, at[before, 0], at[far, 0], at_x(1)),
+                (11, at[after, 1], at[far, 1], at_x(NX - 1)),
+            ]
 
     def tile_copy(k, t):
         source = full.at[t, mp_chip if k == 2 else mp]
         return remote(source, source, s.img.send.at[k, t], s.img.recv.at[k, t], chip if k == 0 else other)
 
-    text_gather = Gather(s.texts)
+    text_gather = TextGather(s.texts)
     for t in range(AHEAD):
         tile_copy(0, t).start()
         tile_copy(1, t).start()
@@ -324,7 +340,7 @@
         arrived(parts.at[source], s.part.send.at[k], s.part.recv.at[k], group[k])
     block = parts[0] + parts[1] + parts[2] + parts[3]
     pooled = (jnp.where(first, image_sum[0, 0:2, :], image_sum[1, 0:2, :]) + block) * (1.0 / PATCH)
-    pool_gather = Gather(s.pool)
+    pool_gather = PoolGather(s.pool)
     mine = jnp.where(core == 0, pooled[0:1, :], pooled[1:2, :])
     pooled_high = mine.astype(b16)
     pooled_rest = (mine - pooled_high.astype(f32)).astype(b16)
@@ -333,7 +349,7 @@
     packed = jnp.broadcast_to(rows[0], (4, D))
     for k in range(1, 4):
         packed = jnp.where(order == k, rows[k], packed)
-    s.pool.buf[yh, x, z] = packed.astype(b16)
+    s.pool.buf[x, yh, z] = packed.astype(b16)
     pool_gather.start(0)
 
     scale = scale_ref[0]
@@ -347,7 +363,8 @@
         if values.shape[0] == 2:
             matches = iota((2, BATCH), 1) == iota((2, BATCH), 0) * HALF + slot
         else:
-            matches = iota((BATCH, BATCH), 0) == iota((BATCH, BATCH), 1)
+            at = iota((BATCH, BATCH), 0)
+            matches = (at & 112) + ((at & 7) << 1) + ((at >> 3) & 1) == iota((BATCH, BATCH), 1)
         signs = jnp.where(matches, 1.0, -1.0)
         coef = -signs * jax.nn.sigmoid(-signs * logits)
         weights = (scale * coef).astype(b16)
@@ -414,9 +431,8 @@
             self.refs, self.begin, self.width = refs, begin, width
             self.span = slice(begin, begin + width)
 
-        def send_pair(self, ring):
-            ring.finish()
-            value = ring.total(slice(0, PAIR))
+        def send_pair(self):
+            value = self.last_total()
             for h in range(NH):
                 self.refs.pair.buf[h] = value[24 * h : 24 * h + 24, :]
             sems = self.refs.pair.send.at[0], self.refs.pair.recv.at[0]
@@ -499,11 +515,14 @@
                 ]
                 self.refs.ring.buf[k] = jnp.concatenate(both, axis=0).astype(b16)
 
+        def last_total(self):
+            self.z.finish()
+            return self.z.total(slice(0, PAIR))
+
     class GroupB(Group):
         def __init__(self, refs, begin, width, steps):
             super().__init__(refs, begin, width)
             self.z = Ring(refs.stage, z, NZ, near_z, steps)
-            self.x = Ring(refs.ring, x, NX, near_x, (2, 1) if steps[0] > steps[1] else (1, 2))
 
         def pack(self):
             pack = self.refs.pack
@@ -530,8 +549,24 @@
                 ]
                 self.refs.ring.buf[k] = jnp.concatenate(both, axis=0).astype(b16)
 
-    a = GroupA(s.a, *GROUPS_A[0], (3, 4))
-    b = GroupB(s.b, *GROUPS_B[0], (4, 3))
+        def send_x(self):
+            refs = self.refs.ring
+            for d in range(1, NX):
+                source, sems = refs.buf.at[(x + d) % NX], (refs.send.at[d - 1], refs.recv.at[d - 1])
+                send(source, refs.right.at[d - 1], *sems, at_x(d))
+
+        def last_total(self):
+            refs = self.refs.ring
+            value = refs.buf[x].astype(f32)
+            for d in range(1, NX):
+                arrived(refs.right.at[d - 1], refs.send.at[d - 1], refs.recv.at[d - 1], at_x(d))
+                value += refs.right[d - 1].astype(f32)
+            return value
+
+    a1 = GroupA(s.a[0], *GROUPS_A[0], (3, 4))
+    a2 = GroupA(s.a[1], *GROUPS_A[1], (4, 3))
+    b1 = GroupB(s.b[0], *GROUPS_B[0], (4, 3))
+    b2 = GroupB(s.b[1], *GROUPS_B[1], (3, 4))
 
     pairs = Refs({})
 
@@ -567,43 +602,62 @@
         own_text = mm(chosen, pairs.proj).astype(b16)
         out_texts[...] = mm_nt(own_text, w_text[...]).astype(b16)
 
-    a.first()
-    b.pack()
-    b.z.step(1)
-    a.second()
+    a1.first()
+    a2.first()
+    b1.pack()
+    b1.z.step(1)
+    a1.second()
+    b2.pack()
+    b2.z.step(1)
+    a2.second()
     pool_gather.wait(0)
     pool_gather.start(1)
-    a.third()
-    b.z.step(2)
-    a.combine(x)
-    b.z.step(3)
+    a1.third()
+    b1.z.step(2)
+    a2.third()
+    b2.z.step(2)
+    a1.combine(x)
+    a2.combine(x)
+    b1.z.step(3)
     pool_gather.wait(1)
     pool_gather.start(2)
-    a.finish_x()
-    a.z.step(1)
-    b.z.step(4)
-    a.z.step(2)
-    b.finish_z()
-    b.x.step(1)
-    a.z.step(3)
+    b2.z.step(3)
+    a1.finish_x()
+    a1.z.step(1)
+    b1.z.step(4)
+    a2.finish_x()
+    a2.z.step(1)
+    b2.z.step(4)
+    a1.z.step(2)
+    a2.z.step(2)
+    b1.finish_z()
+    b1.send_x()
     pool_gather.wait(2)
+    pool_gather.start(3)
+    b2.finish_z()
+    b2.send_x()
+    a1.z.step(3)
+    a2.z.step(3)
+    b1.send_pair()
+    a1.z.step(4)
+    b2.send_pair()
+    a2.z.step(4)
+    pool_gather.wait(3)
     core_sems = s.core.send.at[0], s.core.recv.at[0]
     send(s.pool.buf, s.pool_other, *core_sems, other)
-    b.x.step(2)
-    a.z.step(4)
+    a1.send_pair()
+    a2.send_pair()
     arrived(s.pool_other, *core_sems, other)
     pairs_1()
-    b.send_pair(b.x)
     pairs_2()
-    a.send_pair(a.z)
     pairs_3()
     pairs_4()
-    b.result()
-    a.result()
+    for group in (b1, b2, a1, a2):
+        group.result()
     for copy in sent:
         copy.wait_send()
-    for gather in (text_gather, pool_gather):
-        gather.drain()
+    text_gather.drain(3)
+    pool_gather.drain(4)
 
     def drain_tiles(t, carry):
         for k in range(3):
@@ -614,12 +668,8 @@
 
 
 def hand_on(*refs):
-    sems = refs[8]
-    copies = [pltpu.make_async_copy(refs[k], refs[4 + k], sems.at[k]) for k in range(4)]
-    for copy in copies:
-        copy.start()
-    for copy in copies:
-        copy.wait()
+    for k in range(4):
+        refs[4 + k][...] = refs[k][...]
 
 
 def shards(images, ln_gain, w_in, b_in, w_out, texts, w_text, b_text, logit_scale, logit_bias):
@@ -657,7 +707,7 @@
         image_sum=V((2, 8, D), f32),
         product=V((2, D, D), f32),
         parts=V((NM, 2, D), f32),
-        pool_other=V((NH, NX, NZ, 4, D), b16),
+        pool_other=V((NX, NH, NZ, 4, D), b16),
         text_rows=V((BATCH, D), b16),
         text_emb=V((BATCH, D), b16),
         text_unit=V((BATCH, D), f32),
@@ -667,33 +717,37 @@
         img=with_sems((3, 2 * TILES)),
         part=with_sems((3,)),
         core=with_sems((1,)),
-        texts=with_sems((11,), buf=V((NH, NX, NZ, 2, D), f32)),
-        pool=with_sems((11,), buf=V((NH, NX, NZ, 4, D), b16)),
+        texts=with_sems((11,), buf=V((NX, NZ, NH, 2, D), f32)),
+        pool=with_sems((12,), buf=V((NX, NH, NZ, 4, D), b16)),
     )
-    width = GROUPS_A[0][1]
-    stage = with_sems(
-        (6,),
-        buf=V((NX, OWN, width), b16),
-        right=V((3, 144, width), b16),
-        left=V((3, 144, width), b16),
-    )
-    refs.update(
-        a=dict(
+    def group_a(width, steps):
+        stage = with_sems(
+            (6,),
+            buf=V((NX, OWN, width), b16),
+            right=V((3, 144, width), b16),
+            left=V((3, 144, width), b16),
+        )
+        return dict(
             stage=stage,
             sum=V((OWN + 8, width), f32),
-            ring=ring(b16, (NZ, PAIR), (3, 4), width),
+            ring=ring(b16, (NZ, PAIR), steps, width),
             pair=pair(width),
         )
-    )
-    width = GROUPS_B[0][1]
-    refs.update(
-        b=dict(
+
+    def group_b(width, steps):
+        return dict(
             pack=V((144, width), f32),
-            stage=ring(b16, (NZ, 144), (4, 3), width),
+            stage=ring(b16, (NZ, 144), steps, width),
             sum=V((152, width), f32),
-            ring=ring(b16, (NX, PAIR), (2, 1), width),
+            ring=with_sems(
+                (NX - 1,), buf=V((NX, PAIR, width), b16), right=V((NX - 1, PAIR, width), b16)
+            ),
             pair=pair(width),
         )
+
+    refs.update(
+        a=[group_a(GROUPS_A[0][1], (3, 4)), group_a(GROUPS_A[1][1], (4, 3))],
+        b=[group_b(GROUPS_B[0][1], (4, 3)), group_b(GROUPS_B[1][1], (3, 4))],
     )
     out_shape = [
         jax.ShapeDtypeStruct((ROWS, HID), f32),
@@ -725,9 +779,8 @@
     grad_in, grad_out, grad_text, grad_texts = pl.pallas_call(
         hand_on,
         out_shape=out_shape,
-        in_specs=[hbm] * 4,
-        out_specs=[hbm] * 4,
-        scratch_shapes=[dma((4,))],
+        in_specs=[vmem] * 4,
+        out_specs=[vmem] * 4,
         compiler_params=pltpu.CompilerParams(vmem_limit_bytes=58 << 20),
     )(*results)
     return grad_in, grad_out.T, grad_text, grad_texts

time: 99 us -> 86.6 us (0.87); the launches traced: 97.6 us -> 86.4 us
  Pallas kernels: 95.7 us -> 84.5 us
    pallas_call x1, Pallas kernels: 11.3 us -> 1.74 us  [shards(): pl.pallas_call(hand_on, out_shape=out_shape, in_specs=[vmem] * 4, out_spe...]
    pallas_call x1, Pallas kernels: 84.3 us -> 82.7 us  [shards(): pl.pallas_call(kernel, out_shape=out_shape, in_specs=[vmem] * 5 + [smem]...]
where the time goes in v3:
time: 86.6 us; the launch traced here: 86.4 us
  Pallas kernels  84.5 us (98%)
  between operations  1.93 us (2%)
    pallas_call x1, Pallas kernels, shards(): pl.pallas_call(kernel, out_shape=out_shape, in_specs=[vmem] * 5 + [smem]...  82.7 us
    pallas_call x1, Pallas kernels, shards(): pl.pallas_call(hand_on, out_shape=out_shape, in_specs=[vmem] * 4, out_spe...  1.74 us

profile of v3, /device:TPU:8, one launch (start us, length us, event | category | flops | bytes accessed | tf_op | source)
XLA Modules:
  0.0 86.4 jit_solution(15249480257459115926)
XLA Ops:
  1.9 82.7 %shard_map.129 = (f32[18,1076]{1,0:T(8,128)}, f32[18,1076]{1,0:T(8,128)}, f32[18,1152]{1,0:T(8,128)}, bf16[2,1152]{1,0:T(2,128)(2,1)}) custom-call(bf16[2,288,729]{2,1,0:T(8,128)(2,1)} %bitcast.4, f32[1152]{0:T(1024)} %gain_row.1, f32[1076]{0:T(1024)} %bias_in.1, f32[1152]{0:T(1024)} %bias_text.1, bf16[2,1152]{1,0:T(2,128)(2,1)} %texts.1, ...), custom_call_target="tpu_custom_call" | custom-call | tf_op jit(solution)/shard_map/pallas_call | solution.py:758
  84.7 1.7 %shard_map.130 = (f32[18,1076]{1,0:T(8,128)}, f32[18,1076]{1,0:T(8,128)}, f32[18,1152]{1,0:T(8,128)}, bf16[2,1152]{1,0:T(2,128)(2,1)}) custom-call(f32[18,1076]{1,0:T(8,128)} %get-tuple-element.12.refs_0_, f32[18,1076]{1,0:T(8,128)} %get-tuple-element.13.refs_1_, f32[18,1152]{1,0:T(8,128)} %get-tuple-element.14.refs_2_, ...), custom_call_target="tpu_custom_call" | custom-call | tf_op jit(solution)/shard_map/pallas_call | solution.py:779

commit v4 on v3

--- a/solution.py
+++ b/solution.py
@@ -90,9 +90,10 @@
     s,
 ):
     s = Refs(s)
-    w_in, w_tail, w_out, w_text = s.w_in, s.w_tail, s.w_out, s.w_text
+    w_in, w_pad, w_out, w_text = s.w_in, s.w_pad, s.w_out, s.w_text
     full, normed, slopes, product = s.full, s.normed, s.slopes, s.product
     act_sum, image_sum, grad_act, parts = s.act_sum, s.image_sum, s.grad_act, s.parts
+    act_lanes, before = s.act_lanes, s.before
 
     dp = lax.axis_index("dp")
     mp = lax.axis_index("mp")
@@ -215,7 +216,8 @@
         tile_copy(1, t).start()
     text_gather.start(0)
 
-    product[...] = jnp.zeros_like(product)
+    product[:, :, PADDED:D] = jnp.zeros((2, D, D - PADDED), f32)
+    act_lanes[...] = jnp.zeros_like(act_lanes)
     act_sum[...] = jnp.zeros_like(act_sum)
     image_sum[...] = jnp.zeros_like(image_sum)
     grad_act[...] = jnp.zeros_like(grad_act)
@@ -234,17 +236,18 @@
     tail = (iota((PADDED - whole, HID - whole), 0) == iota((PADDED - whole, HID - whole), 1)).astype(
         b16
     )
-    w_tail[...] = mm(tail, w_in[whole:HID, :]).astype(b16)
-
-    def add_product(t):
-        i = t // TILES
+    w_pad[0:whole, :] = w_in[0:whole, :]
+    w_pad[whole:PADDED, :] = mm(tail, w_in[whole:HID, :]).astype(b16)
+
+    def multiply(i):
         for begin, width in chunks:
             span = slice(begin, begin + width)
-            product[i, :, span] += mm_nt(normed[t], slopes[t, span, :])
+            product[i, :, span] = mm_nt(normed[i], slopes[i, span, :])
 
     def work_on(t):
         i = t // TILES
         j = t % TILES
+        patches = pl.ds(pl.multiple_of(j * TILE, TILE), TILE)
         for h in range(TILE // 128):
             lanes = slice(128 * h, 128 * h + 128)
             total = jnp.zeros((1, 128), f32)
@@ -259,17 +262,18 @@
             for m in range(NM):
                 rows = slice(OWN * m, OWN * m + OWN)
                 centered = full[t, m, :, lanes].astype(f32) - mean
-                normed[t, rows, lanes] = (centered * factor * s.gain_col[rows, :]).astype(b16)
-        valid = (iota((8, TILE), 1) + j * TILE < PATCH).astype(b16)
-        image_sum[i] += mm_nt(valid, full[t].reshape(D, TILE))
+                there = pl.ds(pl.multiple_of(j * TILE + 128 * h, 128), 128)
+                normed[i, rows, there] = (centered * factor * s.gain_col[rows, :]).astype(b16)
+        image_sum[i] += mm_nt(jnp.ones((8, TILE), b16), full[t].reshape(D, TILE))
+        before[...] = mm(w_pad[...], normed[i, :, patches])
+        valid = (iota((1, TILE), 1) + j * TILE < PATCH).astype(f32)
         for begin, width in chunks:
             span = slice(begin, begin + width)
             bias = s.bias_col[span, :]
-            weight = w_in[span, :] if begin < whole else w_tail[...]
-            before = mm(weight, normed[t]) + jnp.concatenate([bias, bias], axis=1)
-            act, slope = gelu_and_slope(before)
-            slopes[t, span, :] = slope.astype(b16)
-            act_sum[i, :, span] += mm_nt(valid, act.astype(b16))
+            act, slope = gelu_and_slope(before[span, :] + jnp.concatenate([bias, bias], axis=1))
+            slopes[i, span, patches] = slope.astype(b16)
+            act = act * valid
+            act_lanes[i, span, :] += act[:, 0:128] + act[:, 128:TILE]
 
     def project_texts():
         loads[2].wait()
@@ -293,9 +297,9 @@
             tile_copy(0, t + AHEAD).start()
             tile_copy(1, t + AHEAD).start()
 
-        @pl.when(t > 0)
+        @pl.when(t == TILES)
         def _():
-            add_product(t - 1)
+            multiply(0)
 
         @pl.when(t == 1)
         def _():
@@ -320,6 +324,10 @@
     lax.fori_loop(0, 2 * TILES, tile_step, 0)
 
     loads[1].wait()
+    ones = jnp.ones((8, 128), b16)
+    for i in range(2):
+        high, middle, low = three_parts(act_lanes[i])
+        act_sum[i, :, 0:PADDED] = mm_nt(ones, high) + mm_nt(ones, middle) + mm_nt(ones, low)
     row = iota((8, HID), 0)
     split = three_parts(act_sum[0, :, 0:HID]) + three_parts(act_sum[1, :, 0:HID])
     stacked = jnp.zeros((8, HID), f32)
@@ -335,7 +343,7 @@
     for k, partner in enumerate(group):
         own = parts.at[mp]
         send(own, own, s.part.send.at[k], s.part.recv.at[k], partner)
-    add_product(2 * TILES - 1)
+    multiply(1)
     for k, source in enumerate((mp_chip, mp_core, mp_far)):
         arrived(parts.at[source], s.part.send.at[k], s.part.recv.at[k], group[k])
     block = parts[0] + parts[1] + parts[2] + parts[3]
@@ -375,6 +383,8 @@
 
     own_block, _, _ = block_gradient(pooled)
     grad_act[:, 0:HID] = mm_nt(own_block, w_out[...])
+    pool_gather.wait(0)
+    pool_gather.start(1)
 
     near_z = (at_z(1), at_z(NZ - 1))
     near_x = (at_x(1), at_x(NX - 1))
@@ -591,12 +601,11 @@
         pairs.proj = ((grad_text - unit * along) / s.text_norm[:, 0:1]).astype(b16)
 
     def pairs_3():
-        acts = jnp.concatenate(
-            [s.pool.buf[:, :, :, 2 + r, 0:HID].reshape(HALF, HID) for r in range(2)], axis=0
-        )
-        out_out[...] = mm_tn(pairs.columns, acts)
+        for r in range(2):
+            s.acts[HALF * r : HALF * r + HALF, :] = s.pool.buf[:, :, :, 2 + r, :].reshape(HALF, D)
 
     def pairs_4():
+        out_out[...] = mm_tn(pairs.columns, s.acts[:, 0:HID])
         out_text[...] = mm_tn(pairs.features, pairs.proj)
         chosen = (iota((2, BATCH), 1) == iota((2, BATCH), 0) * HALF + slot).astype(b16)
         own_text = mm(chosen, pairs.proj).astype(b16)
@@ -610,47 +619,45 @@
     b2.pack()
     b2.z.step(1)
     a2.second()
-    pool_gather.wait(0)
-    pool_gather.start(1)
     a1.third()
     b1.z.step(2)
     a2.third()
     b2.z.step(2)
+    pool_gather.wait(1)
+    pool_gather.start(2)
     a1.combine(x)
     a2.combine(x)
     b1.z.step(3)
-    pool_gather.wait(1)
-    pool_gather.start(2)
     b2.z.step(3)
     a1.finish_x()
     a1.z.step(1)
     b1.z.step(4)
     a2.finish_x()
     a2.z.step(1)
+    pool_gather.wait(2)
+    pool_gather.start(3)
     b2.z.step(4)
     a1.z.step(2)
     a2.z.step(2)
     b1.finish_z()
     b1.send_x()
-    pool_gather.wait(2)
-    pool_gather.start(3)
     b2.finish_z()
     b2.send_x()
+    pool_gather.wait(3)
+    core_sems = s.core.send.at[0], s.core.recv.at[0]
+    send(s.pool.buf, s.pool_other, *core_sems, other)
     a1.z.step(3)
     a2.z.step(3)
+    pairs_3()
     b1.send_pair()
     a1.z.step(4)
     b2.send_pair()
     a2.z.step(4)
-    pool_gather.wait(3)
-    core_sems = s.core.send.at[0], s.core.recv.at[0]
-    send(s.pool.buf, s.pool_other, *core_sems, other)
+    arrived(s.pool_other, *core_sems, other)
+    pairs_1()
     a1.send_pair()
     a2.send_pair()
-    arrived(s.pool_other, *core_sems, other)
-    pairs_1()
     pairs_2()
-    pairs_3()
     pairs_4()
     for group in (b1, b2, a1, a2):
         group.result()
@@ -694,20 +701,23 @@
 
     refs = dict(
         w_in=V((HID, D), b16),
-        w_tail=V((PADDED - HID // TILE * TILE, D), b16),
+        w_pad=V((PADDED, D), b16),
+        before=V((PADDED, TILE), f32),
+        act_lanes=V((2, PADDED, 128), f32),
         w_out=V((HID, D), b16),
         w_text=V((D, D), b16),
         gain_col=V((D, 128), f32),
         bias_col=V((D, 128), f32),
         row_pad=V((1, D), f32),
         full=V((2 * TILES, NM, OWN, TILE), b16),
-        normed=V((2 * TILES, D, TILE), b16),
-        slopes=V((2 * TILES, PADDED, TILE), b16),
+        normed=V((2, D, TILES * TILE), b16),
+        slopes=V((2, PADDED, TILES * TILE), b16),
         act_sum=V((2, 8, D), f32),
         image_sum=V((2, 8, D), f32),
         product=V((2, D, D), f32),
         parts=V((NM, 2, D), f32),
         pool_other=V((NX, NH, NZ, 4, D), b16),
+        acts=V((BATCH, D), b16),
         text_rows=V((BATCH, D), b16),
         text_emb=V((BATCH, D), b16),
         text_unit=V((BATCH, D), f32),

time: 86.6 us -> 89.8 us (1.037)
  Pallas kernels: 84.5 us -> 87.7 us
    pallas_call x1, Pallas kernels: 82.7 us -> 86 us  [shards(): pl.pallas_call(kernel, out_shape=out_shape, in_specs=[vmem] * 5 + [smem]...]
where the time goes in v4:
time: 89.8 us; the launch traced here: 89.7 us
  Pallas kernels  87.7 us (98%)
  between operations  1.93 us (2%)
    pallas_call x1, Pallas kernels, shards(): pl.pallas_call(kernel, out_shape=out_shape, in_specs=[vmem] * 5 + [smem]...  86 us

profile of v4, /device:TPU:8, one launch (start us, length us, event | category | flops | bytes accessed | tf_op | source)
XLA Modules:
  0.0 89.7 jit_solution(70213429132835360)
XLA Ops:
  1.9 86.0 %shard_map.129 = (f32[18,1076]{1,0:T(8,128)}, f32[18,1076]{1,0:T(8,128)}, f32[18,1152]{1,0:T(8,128)}, bf16[2,1152]{1,0:T(2,128)(2,1)}) custom-call(bf16[2,288,729]{2,1,0:T(8,128)(2,1)} %bitcast.4, f32[1152]{0:T(1024)} %gain_row.1, f32[1076]{0:T(1024)} %bias_in.1, f32[1152]{0:T(1024)} %bias_text.1, bf16[2,1152]{1,0:T(2,128)(2,1)} %texts.1, ...), custom_call_target="tpu_custom_call" | custom-call | tf_op jit(solution)/shard_map/pallas_call | solution.py:768
  87.9 1.7 %shard_map.130 = (f32[18,1076]{1,0:T(8,128)}, f32[18,1076]{1,0:T(8,128)}, f32[18,1152]{1,0:T(8,128)}, bf16[2,1152]{1,0:T(2,128)(2,1)}) custom-call(f32[18,1076]{1,0:T(8,128)} %get-tuple-element.12.refs_0_, f32[18,1076]{1,0:T(8,128)} %get-tuple-element.13.refs_1_, f32[18,1152]{1,0:T(8,128)} %get-tuple-element.14.refs_2_, ...), custom_call_target="tpu_custom_call" | custom-call | tf_op jit(solution)/shard_map/pallas_call | solution.py:789

commit v5 on v3

--- a/solution.py
+++ b/solution.py
@@ -73,11 +73,11 @@
 
 
 def kernel(
-    images,
-    gain_row,
-    bias_in,
-    bias_text,
-    texts,
+    images_hbm,
+    gain_hbm,
+    bias_hbm,
+    shift_hbm,
+    texts_hbm,
     scale_ref,
     shift_ref,
     w_in_hbm,
@@ -91,6 +91,8 @@
 ):
     s = Refs(s)
     w_in, w_tail, w_out, w_text = s.w_in, s.w_tail, s.w_out, s.w_text
+    images, texts = s.images, s.own_texts
+    gain_row, bias_in, bias_text = s.gain_row, s.bias_in, s.bias_text
     full, normed, slopes, product = s.full, s.normed, s.slopes, s.product
     act_sum, image_sum, grad_act, parts = s.act_sum, s.image_sum, s.grad_act, s.parts
 
@@ -136,13 +138,14 @@
     def arrived(dst, send_sem, recv_sem, device):
         remote(dst, dst, send_sem, recv_sem, device).wait_recv()
 
+    sources = (w_in_hbm, w_out_hbm, w_text_hbm, images_hbm, texts_hbm, gain_hbm, bias_hbm, shift_hbm)
+    targets = (w_in, w_out, w_text, images, texts, gain_row, bias_in, bias_text)
     loads = [
-        pltpu.make_async_copy(w_in_hbm, w_in, s.load_sem.at[0]),
-        pltpu.make_async_copy(w_out_hbm, w_out, s.load_sem.at[1]),
-        pltpu.make_async_copy(w_text_hbm, w_text, s.load_sem.at[2]),
+        pltpu.make_async_copy(source, target, s.load_sem.at[k])
+        for k, (source, target) in enumerate(zip(sources, targets))
     ]
-    for load in loads:
-        load.start()
+    for k in (3, 4, 5, 6, 0, 2, 7, 1):
+        loads[k].start()
 
     barrier = pltpu.get_barrier_semaphore()
     partners = [chip, other, far, at_yh()]
@@ -150,6 +153,7 @@
     for partner in partners:
         pl.semaphore_signal(barrier, inc=1, device_id=partner, device_id_type=MESH)
 
+    loads[3].wait()
     for i in range(2):
         for j in range(TILES):
             begin = j * TILE
@@ -157,6 +161,7 @@
             if width < TILE:
                 full[i * TILES + j, mp] = jnp.zeros((OWN, TILE), b16)
             full[i * TILES + j, mp, :, 0:width] = images[i, :, begin : begin + width]
+    loads[4].wait()
     s.texts.buf[x, z, yh] = texts[...].astype(f32)
 
     pl.semaphore_wait(barrier, len(partners))
@@ -219,6 +224,8 @@
     act_sum[...] = jnp.zeros_like(act_sum)
     image_sum[...] = jnp.zeros_like(image_sum)
     grad_act[...] = jnp.zeros_like(grad_act)
+    loads[5].wait()
+    loads[6].wait()
     diagonal = iota((128, 128), 0) == iota((128, 128), 1)
     row_pad = s.row_pad
     for row, column, width in ((gain_row, s.gain_col, D), (bias_in, s.bias_col, HID)):
@@ -273,6 +280,7 @@
 
     def project_texts():
         loads[2].wait()
+        loads[7].wait()
         for r in range(2):
             s.text_rows[HALF * r : HALF * r + HALF, :] = (
                 s.texts.buf[:, :, :, r, :].reshape(HALF, D).astype(b16)
@@ -284,39 +292,45 @@
         s.text_unit[...] = unit
         s.text_emb[...] = unit.astype(b16)
 
-    def tile_step(t, carry):
+    def pass_on(t):
         arrived(full.at[t, mp_chip], s.img.send.at[0, t], s.img.recv.at[0, t], chip)
         tile_copy(2, t).start()
+
+    def tile_step(t, carry):
+        @pl.when(t < 2 * TILES - 1)
+        def _():
+            pass_on(t + 1)
 
         @pl.when(t < 2 * TILES - AHEAD)
         def _():
             tile_copy(0, t + AHEAD).start()
             tile_copy(1, t + AHEAD).start()
 
+        @pl.when(t == 0)
+        def _():
+            text_gather.wait(0)
+            text_gather.start(1)
+
+        @pl.when(t == 2)
+        def _():
+            text_gather.wait(1)
+            text_gather.start(2)
+
+        @pl.when(t == 4)
+        def _():
+            text_gather.wait(2)
+            project_texts()
+
         @pl.when(t > 0)
         def _():
             add_product(t - 1)
-
-        @pl.when(t == 1)
-        def _():
-            text_gather.wait(0)
-            text_gather.start(1)
-
-        @pl.when(t == 3)
-        def _():
-            text_gather.wait(1)
-            text_gather.start(2)
-
-        @pl.when(t == 5)
-        def _():
-            text_gather.wait(2)
-            project_texts()
 
         arrived(full.at[t, mp_core], s.img.send.at[1, t], s.img.recv.at[1, t], other)
         arrived(full.at[t, mp_far], s.img.send.at[2, t], s.img.recv.at[2, t], other)
         work_on(t)
         return carry
 
+    pass_on(0)
     lax.fori_loop(0, 2 * TILES, tile_step, 0)
 
     loads[1].wait()
@@ -375,6 +389,8 @@
 
     own_block, _, _ = block_gradient(pooled)
     grad_act[:, 0:HID] = mm_nt(own_block, w_out[...])
+    pool_gather.wait(0)
+    pool_gather.start(1)
 
     near_z = (at_z(1), at_z(NZ - 1))
     near_x = (at_x(1), at_x(NX - 1))
@@ -591,12 +607,11 @@
         pairs.proj = ((grad_text - unit * along) / s.text_norm[:, 0:1]).astype(b16)
 
     def pairs_3():
-        acts = jnp.concatenate(
-            [s.pool.buf[:, :, :, 2 + r, 0:HID].reshape(HALF, HID) for r in range(2)], axis=0
-        )
-        out_out[...] = mm_tn(pairs.columns, acts)
+        for r in range(2):
+            s.acts[HALF * r : HALF * r + HALF, :] = s.pool.buf[:, :, :, 2 + r, :].reshape(HALF, D)
 
     def pairs_4():
+        out_out[...] = mm_tn(pairs.columns, s.acts[:, 0:HID])
         out_text[...] = mm_tn(pairs.features, pairs.proj)
         chosen = (iota((2, BATCH), 1) == iota((2, BATCH), 0) * HALF + slot).astype(b16)
         own_text = mm(chosen, pairs.proj).astype(b16)
@@ -610,47 +625,45 @@
     b2.pack()
     b2.z.step(1)
     a2.second()
-    pool_gather.wait(0)
-    pool_gather.start(1)
     a1.third()
     b1.z.step(2)
     a2.third()
     b2.z.step(2)
+    pool_gather.wait(1)
+    pool_gather.start(2)
     a1.combine(x)
     a2.combine(x)
     b1.z.step(3)
-    pool_gather.wait(1)
-    pool_gather.start(2)
     b2.z.step(3)
     a1.finish_x()
     a1.z.step(1)
     b1.z.step(4)
     a2.finish_x()
     a2.z.step(1)
+    pool_gather.wait(2)
+    pool_gather.start(3)
     b2.z.step(4)
     a1.z.step(2)
     a2.z.step(2)
     b1.finish_z()
     b1.send_x()
-    pool_gather.wait(2)
-    pool_gather.start(3)
     b2.finish_z()
     b2.send_x()
+    pool_gather.wait(3)
+    core_sems = s.core.send.at[0], s.core.recv.at[0]
+    send(s.pool.buf, s.pool_other, *core_sems, other)
     a1.z.step(3)
     a2.z.step(3)
+    pairs_3()
     b1.send_pair()
     a1.z.step(4)
     b2.send_pair()
     a2.z.step(4)
-    pool_gather.wait(3)
-    core_sems = s.core.send.at[0], s.core.recv.at[0]
-    send(s.pool.buf, s.pool_other, *core_sems, other)
+    arrived(s.pool_other, *core_sems, other)
+    pairs_1()
     a1.send_pair()
     a2.send_pair()
-    arrived(s.pool_other, *core_sems, other)
-    pairs_1()
     pairs_2()
-    pairs_3()
     pairs_4()
     for group in (b1, b2, a1, a2):
         group.result()
@@ -708,12 +721,18 @@
         product=V((2, D, D), f32),
         parts=V((NM, 2, D), f32),
         pool_other=V((NX, NH, NZ, 4, D), b16),
+        acts=V((BATCH, D), b16),
         text_rows=V((BATCH, D), b16),
         text_emb=V((BATCH, D), b16),
         text_unit=V((BATCH, D), f32),
         text_norm=V((BATCH, 128), f32),
         grad_act=V((2, D), f32),
-        load_sem=dma((3,)),
+        load_sem=dma((8,)),
+        images=V((2, OWN, PATCH), b16),
+        own_texts=V((2, D), b16),
+        gain_row=V((D,), f32),
+        bias_in=V((HID,), f32),
+        bias_text=V((D,), f32),
         img=with_sems((3, 2 * TILES)),
         part=with_sems((3,)),
         core=with_sems((1,)),
@@ -758,7 +777,7 @@
     results = pl.pallas_call(
         kernel,
         out_shape=out_shape,
-        in_specs=[vmem] * 5 + [smem] * 2 + [hbm] * 3,
+        in_specs=[hbm] * 5 + [smem] * 2 + [hbm] * 3,
         out_specs=[vmem] * 4,
         scratch_shapes=[refs],
         compiler_params=pltpu.CompilerParams(

time: 86.6 us -> 93 us (1.074); the launches traced: 86.4 us -> 91.5 us
  Pallas kernels: 84.5 us -> 89.5 us
    pallas_call x1, Pallas kernels: 82.7 us -> 87.8 us  [shards(): pl.pallas_call(kernel, out_shape=out_shape, in_specs=[hbm] * 5 + [smem] *...]
where the time goes in v5:
time: 93 us; the launch traced here: 91.5 us
  Pallas kernels  89.5 us (96%)
  between operations  1.93 us (2%)
    pallas_call x1, Pallas kernels, shards(): pl.pallas_call(kernel, out_shape=out_shape, in_specs=[hbm] * 5 + [smem] *...  87.8 us

profile of v5, /device:TPU:8, one launch (start us, length us, event | category | flops | bytes accessed | tf_op | source)
XLA Modules:
  0.0 91.5 jit_solution(8426638839071686334)
XLA Ops:
  1.9 87.8 %shard_map.129 = (f32[18,1076]{1,0:T(8,128)}, f32[18,1076]{1,0:T(8,128)}, f32[18,1152]{1,0:T(8,128)}, bf16[2,1152]{1,0:T(2,128)(2,1)}) custom-call(bf16[2,288,729]{2,1,0:T(8,128)(2,1)} %bitcast.4, f32[1152]{0:T(1024)} %gain_hbm.1, f32[1076]{0:T(1024)} %bias_hbm.1, f32[1152]{0:T(1024)} %shift_hbm.1, bf16[2,1152]{1,0:T(2,128)(2,1)} %texts_hbm.1, ...), custom_call_target="tpu_custom_call" | custom-call | tf_op jit(solution)/shard_map/pallas_call | solution.py:777
  89.7 1.7 %shard_map.130 = (f32[18,1076]{1,0:T(8,128)}, f32[18,1076]{1,0:T(8,128)}, f32[18,1152]{1,0:T(8,128)}, bf16[2,1152]{1,0:T(2,128)(2,1)}) custom-call(f32[18,1076]{1,0:T(8,128)} %get-tuple-element.12.refs_0_, f32[18,1076]{1,0:T(8,128)} %get-tuple-element.13.refs_1_, f32[18,1152]{1,0:T(8,128)} %get-tuple-element.14.refs_2_, ...), custom_call_target="tpu_custom_call" | custom-call | tf_op jit(solution)/shard_map/pallas_call | solution.py:798

commit v6 on v3

--- a/solution.py
+++ b/solution.py
@@ -20,7 +20,6 @@
 PAIR = 48
 GROUPS_A = ((0, 384), (384, 256))
 GROUPS_B = ((640, 256), (896, 256))
-AHEAD = 3
 PADDED = 1088
 BATCH = 128
 HALF = 64
@@ -73,11 +72,11 @@
 
 
 def kernel(
-    images,
-    gain_row,
-    bias_in,
-    bias_text,
-    texts,
+    images_hbm,
+    gain_hbm,
+    bias_hbm,
+    shift_hbm,
+    texts_hbm,
     scale_ref,
     shift_ref,
     w_in_hbm,
@@ -91,6 +90,8 @@
 ):
     s = Refs(s)
     w_in, w_tail, w_out, w_text = s.w_in, s.w_tail, s.w_out, s.w_text
+    images, texts = s.images, s.own_texts
+    gain_row, bias_in, bias_text = s.gain_row, s.bias_in, s.bias_text
     full, normed, slopes, product = s.full, s.normed, s.slopes, s.product
     act_sum, image_sum, grad_act, parts = s.act_sum, s.image_sum, s.grad_act, s.parts
 
@@ -136,13 +137,14 @@
     def arrived(dst, send_sem, recv_sem, device):
         remote(dst, dst, send_sem, recv_sem, device).wait_recv()
 
+    sources = (w_in_hbm, w_out_hbm, w_text_hbm, images_hbm, texts_hbm, gain_hbm, bias_hbm, shift_hbm)
+    targets = (w_in, w_out, w_text, images, texts, gain_row, bias_in, bias_text)
     loads = [
-        pltpu.make_async_copy(w_in_hbm, w_in, s.load_sem.at[0]),
-        pltpu.make_async_copy(w_out_hbm, w_out, s.load_sem.at[1]),
-        pltpu.make_async_copy(w_text_hbm, w_text, s.load_sem.at[2]),
+        pltpu.make_async_copy(source, target, s.load_sem.at[k])
+        for k, (source, target) in enumerate(zip(sources, targets))
     ]
-    for load in loads:
-        load.start()
+    for k in (3, 4, 5, 6, 0):
+        loads[k].start()
 
     barrier = pltpu.get_barrier_semaphore()
     partners = [chip, other, far, at_yh()]
@@ -150,6 +152,7 @@
     for partner in partners:
         pl.semaphore_signal(barrier, inc=1, device_id=partner, device_id_type=MESH)
 
+    loads[3].wait()
     for i in range(2):
         for j in range(TILES):
             begin = j * TILE
@@ -157,6 +160,7 @@
             if width < TILE:
                 full[i * TILES + j, mp] = jnp.zeros((OWN, TILE), b16)
             full[i * TILES + j, mp, :, 0:width] = images[i, :, begin : begin + width]
+    loads[4].wait()
     s.texts.buf[x, z, yh] = texts[...].astype(f32)
 
     pl.semaphore_wait(barrier, len(partners))
@@ -209,8 +213,10 @@
         source = full.at[t, mp_chip if k == 2 else mp]
         return remote(source, source, s.img.send.at[k, t], s.img.recv.at[k, t], chip if k == 0 else other)
 
+    for k in (2, 7, 1):
+        loads[k].start()
     text_gather = TextGather(s.texts)
-    for t in range(AHEAD):
+    for t in range(2 * TILES):
         tile_copy(0, t).start()
         tile_copy(1, t).start()
     text_gather.start(0)
@@ -219,6 +225,8 @@
     act_sum[...] = jnp.zeros_like(act_sum)
     image_sum[...] = jnp.zeros_like(image_sum)
     grad_act[...] = jnp.zeros_like(grad_act)
+    loads[5].wait()
+    loads[6].wait()
     diagonal = iota((128, 128), 0) == iota((128, 128), 1)
     row_pad = s.row_pad
     for row, column, width in ((gain_row, s.gain_col, D), (bias_in, s.bias_col, HID)):
@@ -273,6 +281,7 @@
 
     def project_texts():
         loads[2].wait()
+        loads[7].wait()
         for r in range(2):
             s.text_rows[HALF * r : HALF * r + HALF, :] = (
                 s.texts.buf[:, :, :, r, :].reshape(HALF, D).astype(b16)
@@ -288,26 +297,21 @@
         arrived(full.at[t, mp_chip], s.img.send.at[0, t], s.img.recv.at[0, t], chip)
         tile_copy(2, t).start()
 
-        @pl.when(t < 2 * TILES - AHEAD)
-        def _():
-            tile_copy(0, t + AHEAD).start()
-            tile_copy(1, t + AHEAD).start()
-
         @pl.when(t > 0)
         def _():
             add_product(t - 1)
 
-        @pl.when(t == 1)
+        @pl.when(t == 0)
         def _():
             text_gather.wait(0)
             text_gather.start(1)
 
-        @pl.when(t == 3)
+        @pl.when(t == 2)
         def _():
             text_gather.wait(1)
             text_gather.start(2)
 
-        @pl.when(t == 5)
+        @pl.when(t == 4)
         def _():
             text_gather.wait(2)
             project_texts()
@@ -713,7 +717,12 @@
         text_unit=V((BATCH, D), f32),
         text_norm=V((BATCH, 128), f32),
         grad_act=V((2, D), f32),
-        load_sem=dma((3,)),
+        load_sem=dma((8,)),
+        images=V((2, OWN, PATCH), b16),
+        own_texts=V((2, D), b16),
+        gain_row=V((D,), f32),
+        bias_in=V((HID,), f32),
+        bias_text=V((D,), f32),
         img=with_sems((3, 2 * TILES)),
         part=with_sems((3,)),
         core=with_sems((1,)),
@@ -758,7 +767,7 @@
     results = pl.pallas_call(
         kernel,
         out_shape=out_shape,
-        in_specs=[vmem] * 5 + [smem] * 2 + [hbm] * 3,
+        in_specs=[hbm] * 5 + [smem] * 2 + [hbm] * 3,
         out_specs=[vmem] * 4,
         scratch_shapes=[refs],
         compiler_params=pltpu.CompilerParams(

time: 86.6 us -> 98 us (1.13)
  Pallas kernels: 84.5 us -> 96 us
    pallas_call x1, Pallas kernels: 82.7 us -> 94.2 us  [shards(): pl.pallas_call(kernel, out_shape=out_shape, in_specs=[hbm] * 5 + [smem] *...]
where the time goes in v6:
time: 98 us; the launch traced here: 97.9 us
  Pallas kernels  96 us (98%)
  between operations  1.93 us (2%)
    pallas_call x1, Pallas kernels, shards(): pl.pallas_call(kernel, out_shape=out_shape, in_specs=[hbm] * 5 + [smem] *...  94.2 us

profile of v6, /device:TPU:8, one launch (start us, length us, event | category | flops | bytes accessed | tf_op | source)
XLA Modules:
  0.0 97.9 jit_solution(60326672968436851)
XLA Ops:
  1.9 94.2 %shard_map.129 = (f32[18,1076]{1,0:T(8,128)}, f32[18,1076]{1,0:T(8,128)}, f32[18,1152]{1,0:T(8,128)}, bf16[2,1152]{1,0:T(2,128)(2,1)}) custom-call(bf16[2,288,729]{2,1,0:T(8,128)(2,1)} %bitcast.4, f32[1152]{0:T(1024)} %gain_hbm.1, f32[1076]{0:T(1024)} %bias_hbm.1, f32[1152]{0:T(1024)} %shift_hbm.1, bf16[2,1152]{1,0:T(2,128)(2,1)} %texts_hbm.1, ...), custom_call_target="tpu_custom_call" | custom-call | tf_op jit(solution)/shard_map/pallas_call | solution.py:767
  96.2 1.7 %shard_map.130 = (f32[18,1076]{1,0:T(8,128)}, f32[18,1076]{1,0:T(8,128)}, f32[18,1152]{1,0:T(8,128)}, bf16[2,1152]{1,0:T(2,128)(2,1)}) custom-call(f32[18,1076]{1,0:T(8,128)} %get-tuple-element.12.refs_0_, f32[18,1076]{1,0:T(8,128)} %get-tuple-element.13.refs_1_, f32[18,1152]{1,0:T(8,128)} %get-tuple-element.14.refs_2_, ...), custom_call_target="tpu_custom_call" | custom-call | tf_op jit(solution)/shard_map/pallas_call | solution.py:788

commit v7 on v6

--- a/solution.py
+++ b/solution.py
@@ -89,11 +89,12 @@
     s,
 ):
     s = Refs(s)
-    w_in, w_tail, w_out, w_text = s.w_in, s.w_tail, s.w_out, s.w_text
+    w_in, w_pad, w_out, w_text = s.w_in, s.w_pad, s.w_out, s.w_text
     images, texts = s.images, s.own_texts
     gain_row, bias_in, bias_text = s.gain_row, s.bias_in, s.bias_text
     full, normed, slopes, product = s.full, s.normed, s.slopes, s.product
     act_sum, image_sum, grad_act, parts = s.act_sum, s.image_sum, s.grad_act, s.parts
+    act_lanes, before = s.act_lanes, s.before
 
     dp = lax.axis_index("dp")
     mp = lax.axis_index("mp")
@@ -216,17 +217,19 @@
     for k in (2, 7, 1):
         loads[k].start()
     text_gather = TextGather(s.texts)
-    for t in range(2 * TILES):
-        tile_copy(0, t).start()
-        tile_copy(1, t).start()
+    tile_copy(0, 0).start()
+    tile_copy(1, 0).start()
     text_gather.start(0)
 
     product[...] = jnp.zeros_like(product)
+    act_lanes[...] = jnp.zeros_like(act_lanes)
     act_sum[...] = jnp.zeros_like(act_sum)
     image_sum[...] = jnp.zeros_like(image_sum)
     grad_act[...] = jnp.zeros_like(grad_act)
     loads[5].wait()
     loads[6].wait()
+    tile_copy(0, 1).start()
+    tile_copy(1, 1).start()
     diagonal = iota((128, 128), 0) == iota((128, 128), 1)
     row_pad = s.row_pad
     for row, column, width in ((gain_row, s.gain_col, D), (bias_in, s.bias_col, HID)):
@@ -242,7 +245,8 @@
     tail = (iota((PADDED - whole, HID - whole), 0) == iota((PADDED - whole, HID - whole), 1)).astype(
         b16
     )
-    w_tail[...] = mm(tail, w_in[whole:HID, :]).astype(b16)
+    w_pad[0:whole, :] = w_in[0:whole, :]
+    w_pad[whole:PADDED, :] = mm(tail, w_in[whole:HID, :]).astype(b16)
 
     def add_product(t):
         i = t // TILES
@@ -268,16 +272,16 @@
                 rows = slice(OWN * m, OWN * m + OWN)
                 centered = full[t, m, :, lanes].astype(f32) - mean
                 normed[t, rows, lanes] = (centered * factor * s.gain_col[rows, :]).astype(b16)
-        valid = (iota((8, TILE), 1) + j * TILE < PATCH).astype(b16)
-        image_sum[i] += mm_nt(valid, full[t].reshape(D, TILE))
+        image_sum[i] += mm_nt(jnp.ones((8, TILE), b16), full[t].reshape(D, TILE))
+        before[...] = mm(w_pad[...], normed[t])
+        valid = (iota((1, TILE), 1) + j * TILE < PATCH).astype(f32)
         for begin, width in chunks:
             span = slice(begin, begin + width)
             bias = s.bias_col[span, :]
-            weight = w_in[span, :] if begin < whole else w_tail[...]
-            before = mm(weight, normed[t]) + jnp.concatenate([bias, bias], axis=1)
-            act, slope = gelu_and_slope(before)
+            act, slope = gelu_and_slope(before[span, :] + jnp.concatenate([bias, bias], axis=1))
             slopes[t, span, :] = slope.astype(b16)
-            act_sum[i, :, span] += mm_nt(valid, act.astype(b16))
+            act = act * valid
+            act_lanes[i, span, :] += act[:, 0:128] + act[:, 128:TILE]
 
     def project_texts():
         loads[2].wait()
@@ -297,6 +301,11 @@
         arrived(full.at[t, mp_chip], s.img.send.at[0, t], s.img.recv.at[0, t], chip)
         tile_copy(2, t).start()
 
+        @pl.when(t < 2 * TILES - 2)
+        def _():
+            tile_copy(0, t + 2).start()
+            tile_copy(1, t + 2).start()
+
         @pl.when(t > 0)
         def _():
             add_product(t - 1)
@@ -324,6 +333,10 @@
     lax.fori_loop(0, 2 * TILES, tile_step, 0)
 
     loads[1].wait()
+    ones = jnp.ones((8, 128), b16)
+    for i in range(2):
+        high, middle, low = three_parts(act_lanes[i])
+        act_sum[i, :, 0:PADDED] = mm_nt(ones, high) + mm_nt(ones, middle) + mm_nt(ones, low)
     row = iota((8, HID), 0)
     split = three_parts(act_sum[0, :, 0:HID]) + three_parts(act_sum[1, :, 0:HID])
     stacked = jnp.zeros((8, HID), f32)
@@ -698,7 +711,9 @@
 
     refs = dict(
         w_in=V((HID, D), b16),
-        w_tail=V((PADDED - HID // TILE * TILE, D), b16),
+        w_pad=V((PADDED, D), b16),
+        before=V((PADDED, TILE), f32),
+        act_lanes=V((2, PADDED, 128), f32),
         w_out=V((HID, D), b16),
         w_text=V((D, D), b16),
         gain_col=V((D, 128), f32),

time: 98 us -> 80 us (0.82)
  Pallas kernels: 96 us -> 77.7 us
    pallas_call x1, Pallas kernels: 94.2 us -> 75.9 us  [shards(): pl.pallas_call(kernel, out_shape=out_shape, in_specs=[hbm] * 5 + [smem] *...]
where the time goes in v7:
time: 80 us; the launch traced here: 79.6 us
  Pallas kernels  77.7 us (97%)
  between operations  1.93 us (2%)
    pallas_call x1, Pallas kernels, shards(): pl.pallas_call(kernel, out_shape=out_shape, in_specs=[hbm] * 5 + [smem] *...  75.9 us
    pallas_call x1, Pallas kernels, shards(): pl.pallas_call(hand_on, out_shape=out_shape, in_specs=[vmem] * 4, out_spe...  1.74 us

profile of v7, /device:TPU:8, one launch (start us, length us, event | category | flops | bytes accessed | tf_op | source)
XLA Modules:
  0.0 79.6 jit_solution(7168461307402644826)
XLA Ops:
  1.9 75.9 %shard_map.129 = (f32[18,1076]{1,0:T(8,128)}, f32[18,1076]{1,0:T(8,128)}, f32[18,1152]{1,0:T(8,128)}, bf16[2,1152]{1,0:T(2,128)(2,1)}) custom-call(bf16[2,288,729]{2,1,0:T(8,128)(2,1)} %bitcast.4, f32[1152]{0:T(1024)} %gain_hbm.1, f32[1076]{0:T(1024)} %bias_hbm.1, f32[1152]{0:T(1024)} %shift_hbm.1, bf16[2,1152]{1,0:T(2,128)(2,1)} %texts_hbm.1, ...), custom_call_target="tpu_custom_call" | custom-call | tf_op jit(solution)/shard_map/pallas_call | solution.py:782
  77.9 1.7 %shard_map.130 = (f32[18,1076]{1,0:T(8,128)}, f32[18,1076]{1,0:T(8,128)}, f32[18,1152]{1,0:T(8,128)}, bf16[2,1152]{1,0:T(2,128)(2,1)}) custom-call(f32[18,1076]{1,0:T(8,128)} %get-tuple-element.12.refs_0_, f32[18,1076]{1,0:T(8,128)} %get-tuple-element.13.refs_1_, f32[18,1152]{1,0:T(8,128)} %get-tuple-element.14.refs_2_, ...), custom_call_target="tpu_custom_call" | custom-call | tf_op jit(solution)/shard_map/pallas_call | solution.py:803

commit v8 on v7

--- a/solution.py
+++ b/solution.py
@@ -254,6 +254,10 @@
             span = slice(begin, begin + width)
             product[i, :, span] += mm_nt(normed[t], slopes[t, span, :])
 
+    def pass_on(t):
+        arrived(full.at[t, mp_chip], s.img.send.at[0, t], s.img.recv.at[0, t], chip)
+        tile_copy(2, t).start()
+
     def work_on(t):
         i = t // TILES
         j = t % TILES
@@ -274,14 +278,23 @@
                 normed[t, rows, lanes] = (centered * factor * s.gain_col[rows, :]).astype(b16)
         image_sum[i] += mm_nt(jnp.ones((8, TILE), b16), full[t].reshape(D, TILE))
         before[...] = mm(w_pad[...], normed[t])
-        valid = (iota((1, TILE), 1) + j * TILE < PATCH).astype(f32)
+
+        @pl.when(t < 2 * TILES - 1)
+        def _():
+            pass_on(t + 1)
+
+        @pl.when(t < 2 * TILES - 3)
+        def _():
+            tile_copy(0, t + 3).start()
+            tile_copy(1, t + 3).start()
+
+        valid = (iota((1, 128), 1) + (j * TILE + 128) < PATCH).astype(f32)
         for begin, width in chunks:
             span = slice(begin, begin + width)
             bias = s.bias_col[span, :]
             act, slope = gelu_and_slope(before[span, :] + jnp.concatenate([bias, bias], axis=1))
             slopes[t, span, :] = slope.astype(b16)
-            act = act * valid
-            act_lanes[i, span, :] += act[:, 0:128] + act[:, 128:TILE]
+            act_lanes[i, span, :] += act[:, 0:128] + act[:, 128:TILE] * valid
 
     def project_texts():
         loads[2].wait()
@@ -298,14 +311,6 @@
         s.text_emb[...] = unit.astype(b16)
 
     def tile_step(t, carry):
-        arrived(full.at[t, mp_chip], s.img.send.at[0, t], s.img.recv.at[0, t], chip)
-        tile_copy(2, t).start()
-
-        @pl.when(t < 2 * TILES - 2)
-        def _():
-            tile_copy(0, t + 2).start()
-            tile_copy(1, t + 2).start()
-
         @pl.when(t > 0)
         def _():
             add_product(t - 1)
@@ -330,6 +335,9 @@
         work_on(t)
         return carry
 
+    pass_on(0)
+    tile_copy(0, 2).start()
+    tile_copy(1, 2).start()
     lax.fori_loop(0, 2 * TILES, tile_step, 0)
 
     loads[1].wait()
@@ -608,12 +616,11 @@
         pairs.proj = ((grad_text - unit * along) / s.text_norm[:, 0:1]).astype(b16)
 
     def pairs_3():
-        acts = jnp.concatenate(
-            [s.pool.buf[:, :, :, 2 + r, 0:HID].reshape(HALF, HID) for r in range(2)], axis=0
-        )
-        out_out[...] = mm_tn(pairs.columns, acts)
+        for r in range(2):
+            s.acts[HALF * r : HALF * r + HALF, :] = s.pool.buf[:, :, :, 2 + r, :].reshape(HALF, D)
 
     def pairs_4():
+        out_out[...] = mm_tn(pairs.columns, s.acts[:, 0:HID])
         out_text[...] = mm_tn(pairs.features, pairs.proj)
         chosen = (iota((2, BATCH), 1) == iota((2, BATCH), 0) * HALF + slot).astype(b16)
         own_text = mm(chosen, pairs.proj).astype(b16)
@@ -637,23 +644,23 @@
     a2.combine(x)
     b1.z.step(3)
     pool_gather.wait(1)
-    pool_gather.start(2)
     b2.z.step(3)
     a1.finish_x()
     a1.z.step(1)
     b1.z.step(4)
     a2.finish_x()
     a2.z.step(1)
+    pool_gather.start(2)
     b2.z.step(4)
     a1.z.step(2)
     a2.z.step(2)
     b1.finish_z()
     b1.send_x()
-    pool_gather.wait(2)
-    pool_gather.start(3)
     b2.finish_z()
     b2.send_x()
     a1.z.step(3)
+    pool_gather.wait(2)
+    pool_gather.start(3)
     a2.z.step(3)
     b1.send_pair()
     a1.z.step(4)
@@ -662,12 +669,12 @@
     pool_gather.wait(3)
     core_sems = s.core.send.at[0], s.core.recv.at[0]
     send(s.pool.buf, s.pool_other, *core_sems, other)
+    pairs_3()
     a1.send_pair()
     a2.send_pair()
     arrived(s.pool_other, *core_sems, other)
     pairs_1()
     pairs_2()
-    pairs_3()
     pairs_4()
     for group in (b1, b2, a1, a2):
         group.result()
@@ -727,6 +734,7 @@
         product=V((2, D, D), f32),
         parts=V((NM, 2, D), f32),
         pool_other=V((NX, NH, NZ, 4, D), b16),
+        acts=V((BATCH, D), b16),
         text_rows=V((BATCH, D), b16),
         text_emb=V((BATCH, D), b16),
         text_unit=V((BATCH, D), f32),

time: 80 us -> 80.1 us (level)
  no operation moved by 1% of the time
where the time goes in v8:
time: 80.1 us; the launch traced here: 79.7 us
  Pallas kernels  77.8 us (97%)
  between operations  1.93 us (2%)
    pallas_call x1, Pallas kernels, shards(): pl.pallas_call(kernel, out_shape=out_shape, in_specs=[hbm] * 5 + [smem] *...  76 us
    pallas_call x1, Pallas kernels, shards(): pl.pallas_call(hand_on, out_shape=out_shape, in_specs=[vmem] * 4, out_spe...  1.74 us

profile of v8, /device:TPU:8, one launch (start us, length us, event | category | flops | bytes accessed | tf_op | source)
XLA Modules:
  0.0 79.7 jit_solution(318279838272565890)
XLA Ops:
  1.9 76.0 %shard_map.129 = (f32[18,1076]{1,0:T(8,128)}, f32[18,1076]{1,0:T(8,128)}, f32[18,1152]{1,0:T(8,128)}, bf16[2,1152]{1,0:T(2,128)(2,1)}) custom-call(bf16[2,288,729]{2,1,0:T(8,128)(2,1)} %bitcast.4, f32[1152]{0:T(1024)} %gain_hbm.1, f32[1076]{0:T(1024)} %bias_hbm.1, f32[1152]{0:T(1024)} %shift_hbm.1, bf16[2,1152]{1,0:T(2,128)(2,1)} %texts_hbm.1, ...), custom_call_target="tpu_custom_call" | custom-call | tf_op jit(solution)/shard_map/pallas_call | solution.py:790
  78.0 1.7 %shard_map.130 = (f32[18,1076]{1,0:T(8,128)}, f32[18,1076]{1,0:T(8,128)}, f32[18,1152]{1,0:T(8,128)}, bf16[2,1152]{1,0:T(2,128)(2,1)}) custom-call(f32[18,1076]{1,0:T(8,128)} %get-tuple-element.12.refs_0_, f32[18,1076]{1,0:T(8,128)} %get-tuple-element.13.refs_1_, f32[18,1152]{1,0:T(8,128)} %get-tuple-element.14.refs_2_, ...), custom_call_target="tpu_custom_call" | custom-call | tf_op jit(solution)/shard_map/pallas_call | solution.py:811

commit v9 on v8

--- a/solution.py
+++ b/solution.py
@@ -101,7 +101,7 @@
     x = dp // (NH * NZ)
     yh = (dp // NZ) % NH
     z = dp % NZ
-    slot = (x * NZ + z) * NH + yh
+    slot = x * 32 + z * NH + yh
     yl = mp // 2
     core = mp % 2
     mp_chip = (1 - yl) * 2 + core
@@ -162,7 +162,7 @@
                 full[i * TILES + j, mp] = jnp.zeros((OWN, TILE), b16)
             full[i * TILES + j, mp, :, 0:width] = images[i, :, begin : begin + width]
     loads[4].wait()
-    s.texts.buf[x, z, yh] = texts[...].astype(f32)
+    s.texts.buf[z, yh] = texts[...].astype(f32)
 
     pl.semaphore_wait(barrier, len(partners))
 
@@ -185,30 +185,46 @@
 
     class TextGather(Gather):
         def copies(self, stage):
-            at = self.buf.at
+            at, dense = self.buf.at, s.text_dense.at
             if stage == 0:
-                return [(0, at[x, z, yh], at[x, z, 1 - yh], at_yh())]
+                return [(0, at[z, yh], at[z, 1 - yh], at_yh())]
             if stage == 1:
-                return [(d, at[x, z], at[x, (z + NZ - d) % NZ], at_z(d)) for d in range(1, NZ)]
-            return [(7 + d, at[x], at[(x + NX - d) % NX], at_x(d)) for d in range(1, NX)]
+                return [(d, at[z], at[(z + NZ - d) % NZ], at_z(d)) for d in range(1, NZ)]
+            return [(7 + d, dense[x], dense[(x + NX - d) % NX], at_x(d)) for d in range(1, NX)]
+
+        def make_dense(self):
+            for r in range(2):
+                s.text_dense[x, r] = self.buf[:, :, r, :].reshape(NZ * NH, D).astype(b16)
 
     class PoolGather(Gather):
         def copies(self, stage):
-            at = self.buf.at
+            at, pool, acts = self.buf.at, s.pool_dense.at, s.act_dense.at
             if stage == 0:
+                return [(d, at[yh, z], at[yh, (z + NZ - d) % NZ], at_z(d)) for d in range(1, NZ)]
+            if stage == 1:
+                return [(0, at[yh], at[1 - yh], at_yh())]
+            before, after, far = (x + NX - 1) % NX, (x + 1) % NX, (x + 2) % NX
+            right, left = at_x(1), at_x(NX - 1)
+            if stage == 2:
                 return [
-                    (d, at[x, yh, z], at[x, yh, (z + NZ - d) % NZ], at_z(d)) for d in range(1, NZ)
+                    (8, pool[x], pool[before], right),
+                    (9, pool[x], pool[after], left),
+                    (10, acts[x], acts[before], right),
+                    (11, acts[x], acts[after], left),
                 ]
-            if stage == 1:
-                return [(0, at[x, yh], at[x, 1 - yh], at_yh())]
-            before, after = (x + NX - 1) % NX, (x + 1) % NX
-            if stage == 2:
-                return [(8, at[x], at[before], at_x(1)), (9, at[x], at[after], at_x(NX - 1))]
-            far = (x + 2) % NX
+            lower, upper = pl.ds(0, 8), pl.ds(8, 8)
             return [
-                (10, at[before, 0], at[far, 0], at_x(1)),
-                (11, at[after, 1], at[far, 1], at_x(NX - 1)),
+                (12, pool[before, lower], pool[far, lower], right),
+                (13, pool[after, upper], pool[far, upper], left),
+                (14, acts[before, 0], acts[far, 0], right),
+                (15, acts[after, 1], acts[far, 1], left),
             ]
+
+        def make_dense(self):
+            rows = [self.buf[:, :, k, :].reshape(NH * NZ, D) for k in range(4)]
+            s.pool_dense[x] = rows[0].astype(f32) + rows[1].astype(f32)
+            s.act_dense[x, 0] = rows[2]
+            s.act_dense[x, 1] = rows[3]
 
     def tile_copy(k, t):
         source = full.at[t, mp_chip if k == 2 else mp]
@@ -299,11 +315,7 @@
     def project_texts():
         loads[2].wait()
         loads[7].wait()
-        for r in range(2):
-            s.text_rows[HALF * r : HALF * r + HALF, :] = (
-                s.texts.buf[:, :, :, r, :].reshape(HALF, D).astype(b16)
-            )
-        projected = mm(s.text_rows[...], w_text[...]) + bias_text[...].reshape(1, D)
+        projected = mm(s.text_dense[...].reshape(BATCH, D), w_text[...]) + bias_text[...].reshape(1, D)
         norm = jnp.sqrt(jnp.sum(projected * projected, axis=1, keepdims=True) + epsilon)
         unit = projected / norm
         s.text_norm[...] = jnp.broadcast_to(norm, (BATCH, 128))
@@ -323,6 +335,7 @@
         @pl.when(t == 2)
         def _():
             text_gather.wait(1)
+            text_gather.make_dense()
             text_gather.start(2)
 
         @pl.when(t == 4)
@@ -374,7 +387,7 @@
     packed = jnp.broadcast_to(rows[0], (4, D))
     for k in range(1, 4):
         packed = jnp.where(order == k, rows[k], packed)
-    s.pool.buf[x, yh, z] = packed.astype(b16)
+    s.pool.buf[yh, z] = packed.astype(b16)
     pool_gather.start(0)
 
     scale = scale_ref[0]
@@ -386,10 +399,11 @@
         emb = unit.astype(b16)
         logits = scale * mm_nt(emb, s.text_emb[...]) + shift
         if values.shape[0] == 2:
-            matches = iota((2, BATCH), 1) == iota((2, BATCH), 0) * HALF + slot
+            matches = iota((2, BATCH), 1) == iota((2, BATCH), 0) * 16 + slot
         else:
             at = iota((BATCH, BATCH), 0)
-            matches = (at & 112) + ((at & 7) << 1) + ((at >> 3) & 1) == iota((BATCH, BATCH), 1)
+            text = (((at >> 4) & 3) << 5) + ((at >> 6) << 4) + ((at & 7) << 1) + ((at >> 3) & 1)
+            matches = text == iota((BATCH, BATCH), 1)
         signs = jnp.where(matches, 1.0, -1.0)
         coef = -signs * jax.nn.sigmoid(-signs * logits)
         weights = (scale * coef).astype(b16)
@@ -596,17 +610,14 @@
     pairs = Refs({})
 
     def pairs_1():
-        halves = []
-        for buf in (s.pool.buf, s.pool_other):
-            both = [buf[:, :, :, r, :].reshape(HALF, D).astype(f32) for r in range(2)]
-            halves.append(both[0] + both[1])
+        halves = [buf[...].reshape(HALF, D) for buf in (s.pool_dense, s.pool_other)]
         lower = jnp.where(core == 0, halves[0], halves[1])
         upper = jnp.where(core == 0, halves[1], halves[0])
         all_pooled = jnp.concatenate([lower, upper], axis=0)
         block, weights, emb = block_gradient(all_pooled)
         pick = (iota((D, ROWS), 0) == iota((D, ROWS), 1) + dp * ROWS).astype(b16)
         pairs.columns = mm(block, pick).astype(b16)
-        pairs.features = mm(s.text_rows[...], pick).astype(b16)
+        pairs.features = mm(s.text_dense[...].reshape(BATCH, D), pick).astype(b16)
         pairs.weights, pairs.emb = weights, emb
 
     def pairs_2():
@@ -615,14 +626,11 @@
         along = jnp.sum(unit * grad_text, axis=1, keepdims=True)
         pairs.proj = ((grad_text - unit * along) / s.text_norm[:, 0:1]).astype(b16)
 
-    def pairs_3():
-        for r in range(2):
-            s.acts[HALF * r : HALF * r + HALF, :] = s.pool.buf[:, :, :, 2 + r, :].reshape(HALF, D)
-
     def pairs_4():
-        out_out[...] = mm_tn(pairs.columns, s.acts[:, 0:HID])
+        acts = [s.act_dense[:, r, :, 0:HID].reshape(HALF, HID) for r in range(2)]
+        out_out[...] = mm_tn(pairs.columns, jnp.concatenate(acts, axis=0))
         out_text[...] = mm_tn(pairs.features, pairs.proj)
-        chosen = (iota((2, BATCH), 1) == iota((2, BATCH), 0) * HALF + slot).astype(b16)
+        chosen = (iota((2, BATCH), 1) == iota((2, BATCH), 0) * 16 + slot).astype(b16)
         own_text = mm(chosen, pairs.proj).astype(b16)
         out_texts[...] = mm_nt(own_text, w_text[...]).astype(b16)
 
@@ -644,6 +652,7 @@
     a2.combine(x)
     b1.z.step(3)
     pool_gather.wait(1)
+    pool_gather.make_dense()
     b2.z.step(3)
     a1.finish_x()
     a1.z.step(1)
@@ -668,8 +677,7 @@
     a2.z.step(4)
     pool_gather.wait(3)
     core_sems = s.core.send.at[0], s.core.recv.at[0]
-    send(s.pool.buf, s.pool_other, *core_sems, other)
-    pairs_3()
+    send(s.pool_dense, s.pool_other, *core_sems, other)
     a1.send_pair()
     a2.send_pair()
     arrived(s.pool_other, *core_sems, other)
@@ -733,9 +741,10 @@
         image_sum=V((2, 8, D), f32),
         product=V((2, D, D), f32),
         parts=V((NM, 2, D), f32),
-        pool_other=V((NX, NH, NZ, 4, D), b16),
-        acts=V((BATCH, D), b16),
-        text_rows=V((BATCH, D), b16),
+        pool_other=V((NX, 16, D), f32),
+        text_dense=V((NX, 2, 16, D), b16),
+        pool_dense=V((NX, 16, D), f32),
+        act_dense=V((NX, 2, 16, D), b16),
         text_emb=V((BATCH, D), b16),
         text_unit=V((BATCH, D), f32),
         text_norm=V((BATCH, 128), f32),
@@ -749,8 +758,8 @@
         img=with_sems((3, 2 * TILES)),
         part=with_sems((3,)),
         core=with_sems((1,)),
-        texts=with_sems((11,), buf=V((NX, NZ, NH, 2, D), f32)),
-        pool=with_sems((12,), buf=V((NX, NH, NZ, 4, D), b16)),
+        texts=with_sems((11,), buf=V((NZ, NH, 2, D), f32)),
+        pool=with_sems((16,), buf=V((NH, NZ, 4, D), b16)),
     )
     def group_a(width, steps):
         stage = with_sems(

time: 80.1 us -> 77.7 us (0.970)
  Pallas kernels: 77.8 us -> 75.2 us
    pallas_call x1, Pallas kernels: 76 us -> 73.5 us  [shards(): pl.pallas_call(kernel, out_shape=out_shape, in_specs=[hbm] * 5 + [smem] *...]
where the time goes in v9:
time: 77.7 us; the launch traced here: 77.1 us
  Pallas kernels  75.2 us (97%)
  between operations  1.93 us (2%)
    pallas_call x1, Pallas kernels, shards(): pl.pallas_call(kernel, out_shape=out_shape, in_specs=[hbm] * 5 + [smem] *...  73.5 us
    pallas_call x1, Pallas kernels, shards(): pl.pallas_call(hand_on, out_shape=out_shape, in_specs=[vmem] * 4, out_spe...  1.74 us

profile of v9, /device:TPU:8, one launch (start us, length us, event | category | flops | bytes accessed | tf_op | source)
XLA Modules:
  0.0 77.1 jit_solution(14047550445026678862)
XLA Ops:
  1.9 73.5 %shard_map.129 = (f32[18,1076]{1,0:T(8,128)}, f32[18,1076]{1,0:T(8,128)}, f32[18,1152]{1,0:T(8,128)}, bf16[2,1152]{1,0:T(2,128)(2,1)}) custom-call(bf16[2,288,729]{2,1,0:T(8,128)(2,1)} %bitcast.4, f32[1152]{0:T(1024)} %gain_hbm.1, f32[1076]{0:T(1024)} %bias_hbm.1, f32[1152]{0:T(1024)} %shift_hbm.1, bf16[2,1152]{1,0:T(2,128)(2,1)} %texts_hbm.1, ...), custom_call_target="tpu_custom_call" | custom-call | tf_op jit(solution)/shard_map/pallas_call | solution.py:799
  75.4 1.7 %shard_map.130 = (f32[18,1076]{1,0:T(8,128)}, f32[18,1076]{1,0:T(8,128)}, f32[18,1152]{1,0:T(8,128)}, bf16[2,1152]{1,0:T(2,128)(2,1)}) custom-call(f32[18,1076]{1,0:T(8,128)} %get-tuple-element.12.refs_0_, f32[18,1076]{1,0:T(8,128)} %get-tuple-element.13.refs_1_, f32[18,1152]{1,0:T(8,128)} %get-tuple-element.14.refs_2_, ...), custom_call_target="tpu_custom_call" | custom-call | tf_op jit(solution)/shard_map/pallas_call | solution.py:820

commit v10 on v9

--- a/solution.py
+++ b/solution.py
@@ -237,7 +237,7 @@
     tile_copy(1, 0).start()
     text_gather.start(0)
 
-    product[...] = jnp.zeros_like(product)
+    product[:, :, PADDED:D] = jnp.zeros((2, D, D - PADDED), f32)
     act_lanes[...] = jnp.zeros_like(act_lanes)
     act_sum[...] = jnp.zeros_like(act_sum)
     image_sum[...] = jnp.zeros_like(image_sum)
@@ -264,11 +264,12 @@
     w_pad[0:whole, :] = w_in[0:whole, :]
     w_pad[whole:PADDED, :] = mm(tail, w_in[whole:HID, :]).astype(b16)
 
-    def add_product(t):
+    def add_product(t, first):
         i = t // TILES
         for begin, width in chunks:
             span = slice(begin, begin + width)
-            product[i, :, span] += mm_nt(normed[t], slopes[t, span, :])
+            term = mm_nt(normed[t], slopes[t, span, :])
+            product[i, :, span] = term if first else product[i, :, span] + term
 
     def pass_on(t):
         arrived(full.at[t, mp_chip], s.img.send.at[0, t], s.img.recv.at[0, t], chip)
@@ -323,9 +324,13 @@
         s.text_emb[...] = unit.astype(b16)
 
     def tile_step(t, carry):
-        @pl.when(t > 0)
+        @pl.when((t > 0) & (t % TILES == 1))
         def _():
-            add_product(t - 1)
+            add_product(t - 1, True)
+
+        @pl.when((t > 0) & (t % TILES != 1))
+        def _():
+            add_product(t - 1, False)
 
         @pl.when(t == 0)
         def _():
@@ -356,8 +361,8 @@
     loads[1].wait()
     ones = jnp.ones((8, 128), b16)
     for i in range(2):
-        high, middle, low = three_parts(act_lanes[i])
-        act_sum[i, :, 0:PADDED] = mm_nt(ones, high) + mm_nt(ones, middle) + mm_nt(ones, low)
+        high, middle, _ = three_parts(act_lanes[i])
+        act_sum[i, :, 0:PADDED] = mm_nt(ones, high) + mm_nt(ones, middle)
     row = iota((8, HID), 0)
     split = three_parts(act_sum[0, :, 0:HID]) + three_parts(act_sum[1, :, 0:HID])
     stacked = jnp.zeros((8, HID), f32)
@@ -373,7 +378,7 @@
     for k, partner in enumerate(group):
         own = parts.at[mp]
         send(own, own, s.part.send.at[k], s.part.recv.at[k], partner)
-    add_product(2 * TILES - 1)
+    add_product(2 * TILES - 1, False)
     for k, source in enumerate((mp_chip, mp_core, mp_far)):
         arrived(parts.at[source], s.part.send.at[k], s.part.recv.at[k], group[k])
     block = parts[0] + parts[1] + parts[2] + parts[3]
@@ -798,7 +803,7 @@
     ]
     results = pl.pallas_call(
         kernel,
-        out_shape=out_shape,
+        out_shape=[V(shape.shape, shape.dtype) for shape in out_shape],
         in_specs=[hbm] * 5 + [smem] * 2 + [hbm] * 3,
         out_specs=[vmem] * 4,
         scratch_shapes=[refs],
@@ -822,7 +827,7 @@
         out_shape=out_shape,
         in_specs=[vmem] * 4,
         out_specs=[vmem] * 4,
-        compiler_params=pltpu.CompilerParams(vmem_limit_bytes=58 << 20),
+        compiler_params=pltpu.CompilerParams(vmem_limit_bytes=4 << 20),
     )(*results)
     return grad_in, grad_out.T, grad_text, grad_texts
 

time: 77.7 us -> 75.8 us (0.976)
  Pallas kernels: 75.2 us -> 73.3 us
    pallas_call x1, Pallas kernels: 1.74 us -> 0.75 us  [shards(): pl.pallas_call(hand_on, out_shape=out_shape, in_specs=[vmem] * 4, out_spe...]
    pallas_call x1, Pallas kernels: 73.5 us -> 72.6 us  [shards(): pl.pallas_call(kernel, out_shape=[V(shape.shape, shape.dtype) for shape i...]
where the time goes in v10:
time: 75.8 us; the launch traced here: 75.3 us
  Pallas kernels  73.3 us (97%)
  between operations  1.93 us (3%)
    pallas_call x1, Pallas kernels, shards(): pl.pallas_call(kernel, out_shape=[V(shape.shape, shape.dtype) for shape i...  72.6 us

profile of v10, /device:TPU:8, one launch (start us, length us, event | category | flops | bytes accessed | tf_op | source)
XLA Modules:
  0.0 75.3 jit_solution(10353708420654552586)
XLA Ops:
  1.9 72.6 %shard_map.129 = (f32[18,1076]{1,0:T(8,128)S(1)}, f32[18,1076]{1,0:T(8,128)S(1)}, f32[18,1152]{1,0:T(8,128)S(1)}, bf16[2,1152]{1,0:T(2,128)(2,1)S(1)}) custom-call(bf16[2,288,729]{2,1,0:T(8,128)(2,1)} %bitcast.4, f32[1152]{0:T(1024)} %gain_hbm.1, f32[1076]{0:T(1024)} %bias_hbm.1, f32[1152]{0:T(1024)} %shift_hbm.1, bf16[2,1152]{1,0:T(2,128)(2,1)} %texts_hbm.1, ...), custom_call_target="tpu_custom_call" | custom-call | tf_op jit(solution)/shard_map/pallas_call | solution.py:804
  74.5 0.7 shard_map.130

commit v11 on v10

--- a/solution.py
+++ b/solution.py
@@ -18,8 +18,8 @@
 TILES = 3
 ROWS = 18
 PAIR = 48
-GROUPS_A = ((0, 384), (384, 256))
-GROUPS_B = ((640, 256), (896, 256))
+GROUPS_A = ((0, 256), (256, 256))
+GROUPS_B = ((512, 384), (896, 256))
 PADDED = 1088
 BATCH = 128
 HALF = 64

time: 75.8 us -> 76.7 us (1.012)
  no operation moved by 1% of the time
where the time goes in v11:
time: 76.7 us; the launch traced here: 75.8 us
  Pallas kernels  73.9 us (96%)
  between operations  1.93 us (3%)
    pallas_call x1, Pallas kernels, shards(): pl.pallas_call(kernel, out_shape=[V(shape.shape, shape.dtype) for shape i...  73.1 us

profile of v11, /device:TPU:8, one launch (start us, length us, event | category | flops | bytes accessed | tf_op | source)
XLA Modules:
  0.0 75.8 jit_solution(8152324636235247688)
XLA Ops:
  1.9 73.1 %shard_map.129 = (f32[18,1076]{1,0:T(8,128)S(1)}, f32[18,1076]{1,0:T(8,128)S(1)}, f32[18,1152]{1,0:T(8,128)S(1)}, bf16[2,1152]{1,0:T(2,128)(2,1)S(1)}) custom-call(bf16[2,288,729]{2,1,0:T(8,128)(2,1)} %bitcast.4, f32[1152]{0:T(1024)} %gain_hbm.1, f32[1076]{0:T(1024)} %bias_hbm.1, f32[1152]{0:T(1024)} %shift_hbm.1, bf16[2,1152]{1,0:T(2,128)(2,1)} %texts_hbm.1, ...), custom_call_target="tpu_custom_call" | custom-call | tf_op jit(solution)/shard_map/pallas_call | solution.py:804
  75.1 0.7 shard_map.130
